TPU v7x, 32 devices: a whole 2x2x4 slice. The times are simulated.
32 devices in a mesh: sub: 4 (over z), cgrp: 8 (over y, x, core).
Axes of the slice: x: 2, y: 2, z: 4, core: 2. Of those that a mesh axis runs over, the one named last changes fastest.
Arguments:
- source: float32 [256, 32768], P('sub', 'cgrp'), may hold values from -7.5 to 7.5
- capacity: float32 [256, 32768], P('sub', 'cgrp'), may hold values from 0.01 to 1
- fd_weights: float32 [256, 32768], P('sub', 'cgrp'), may hold values from 0.02 to 1
- fd_modes: float32 [3, 64, 64], replicated, may hold values from -0.75 to 0.75
- face_modes: float32 [2, 128, 64], replicated, may hold values from -0.75 to 0.75
- coarse_map: int32 [4, 8, 6, 128], P('sub', 'cgrp'), may hold values from 0 to 24575, as said below
- fsai_cols: int32 [192, 8], P(('sub', 'cgrp')), may hold values from 0 to 191
- fsai_blocks: float32 [192, 8, 128, 128], P(('sub', 'cgrp')), may hold values from -0.1875 to 0.1875
Outputs:
- solution: float32 [256, 32768], P('sub', 'cgrp')
- residual: float32 [256, 32768], P('sub', 'cgrp')
Inputs may be any that keep to these rules, and one draw needn't show every extreme that they name: `coarse_map`: entries are numbered by owner: with d = s * 8 + t, face f of subdomain (s, t) takes the entries (6 d + f) * 128 to (6 d + f) * 128 + 127, each once, in an order of its own; except that face 0 of a subdomain with s > 0 takes exactly the entries of face 1 of subdomain (s - 1, t), and face 2 of a subdomain with t > 0 exactly those of face 3 of subdomain (s, t - 1), function k of both sides taking the same entry.
All inputs are finite; a program needn't handle non-finite values.
Results may differ from a plain program's by a relative error of at most 0.0001.
Values sent between devices are 32-bit elements; how exact they have to be, the bound alone decides.
A program may use at most 64 MiB of HBM per device.

v0:
```python
import functools
import jax
import jax.numpy as jnp
from jax import lax
from jax.experimental import pallas as pl
from jax.experimental.pallas import tpu as pltpu
from jax.sharding import PartitionSpec as P

C = 64
T = 32
CH = 8
f32 = jnp.float32
bf16 = jnp.bfloat16
HI = lax.Precision.HIGHEST
MESH = pl.DeviceIdType.MESH


def nn(a, b):
    return lax.dot_general(a, b, (((1,), (0,)), ((), ())), precision=HI, preferred_element_type=f32)


def nt(a, b):
    return lax.dot_general(a, b, (((1,), (1,)), ((), ())), precision=HI, preferred_element_type=f32)


def mm(a, b):
    return lax.dot_general(a, b, (((1,), (0,)), ((), ())), preferred_element_type=f32)


def mmt(a, b):
    return lax.dot_general(a, b, (((1,), (1,)), ((), ())), preferred_element_type=f32)


def split(x):
    hi = x.astype(bf16)
    return hi, (x - hi.astype(f32)).astype(bf16)


def iota(shape, dim):
    return lax.broadcasted_iota(jnp.int32, shape, dim)


def left3(m):
    hi, lo = split(m)
    return jnp.concatenate([hi, lo, hi], axis=1)


def rows3(x):
    hi, lo = split(x)
    return jnp.concatenate([hi, hi, lo], axis=0)


def lanes_weights(k):
    hi, lo = split(k)
    top = jnp.concatenate([hi, lo], axis=1)
    bottom = jnp.concatenate([hi, jnp.zeros_like(lo)], axis=1)
    return jnp.concatenate([top, bottom], axis=0)


def lane_transform(x, w):
    hi, lo = split(x)
    r = mm(jnp.concatenate([hi, lo], axis=1), w)
    return r[:, :128] + r[:, 128:]


def kernel(nsub, ncg, x_any, modes_any, face_any, map_any, cols_any, cap_any, wt_any, blk_any,
           p_out, img_out, alpha_out,
           x_ref, modes_ref, face_ref, map_ref, cols_ref,
           s_ref, z_ref, w_ref, p_ref, cap_ref, blk_ref, sel_ref, am_ref, kw_ref,
           ag_ref, send1_ref, a2s_ref, a2r_ref, pick_ref, spread_ref,
           hi_ref, his_ref, hj_ref, hjs_ref, cs_ref, cr_ref,
           dsem, ag_s, ag_r, a2_s, a2_r, h_s, h_r, c_s, c_r):
    n = nsub * ncg
    s = lax.axis_index("sub")
    t = lax.axis_index("cgrp")
    me = s * ncg + t

    def peer(o):
        d = lax.rem(me + o, n)
        return d, (lax.div(d, ncg), lax.rem(d, ncg))

    early = []
    for k, (src, dst) in enumerate(((face_any, face_ref), (map_any, map_ref), (x_any, x_ref),
                                    (modes_any, modes_ref), (cols_any, cols_ref),
                                    (wt_any, w_ref), (blk_any, blk_ref), (cap_any, cap_ref))):
        early.append(pltpu.make_async_copy(src, dst, dsem.at[k]))
        early[-1].start()
    fcopy, mcopy, xcopy, ocopy, lcopy, wcopy, bcopy, ccopy = early

    def peers(step):
        if n > 32:
            pl.loop(1, n)(step)
        else:
            for o in range(1, n):
                step(o)

    barrier = pltpu.get_barrier_semaphore()

    @pl.loop(1, n)
    def _(o):
        _, dev = peer(o)
        pl.semaphore_signal(barrier, inc=1, device_id=dev, device_id_type=MESH)

    lane = iota((1, 128), 1)
    low = lane < 64
    low32 = jnp.broadcast_to(low, (32, 128))
    low64 = jnp.broadcast_to(low, (64, 128))

    def swap(a):
        return pltpu.roll(a, 64, 1)

    @pl.loop(0, 8)
    def _(c):
        r = iota((128, 512), 0)
        col = iota((128, 512), 1) + c * 512
        hit = ((col >> 6) == (r & 63)) & ((col & 63) == 63 * (r >> 6))
        sel_ref[:, pl.ds(pl.multiple_of(c * 512, 512), 512)] = jnp.where(hit, 1.0, 0.0).astype(bf16)

    fcopy.wait()
    mcopy.wait()
    fm0t = face_ref[0]
    fm1t = face_ref[1]
    r64 = iota((64, 64), 0)
    c64 = iota((64, 64), 1)
    eye64 = jnp.where(r64 == c64, 1.0, 0.0)
    qm = jnp.where(c64 == 2 * (r64 & 31) + (r64 >> 5), 1.0, 0.0)
    dup = jnp.where((iota((64, 128), 1) & 63) == iota((64, 128), 0), 1.0, 0.0)
    dupt = jnp.where((iota((128, 64), 0) & 63) == iota((128, 64), 1), 1.0, 0.0)
    eye128 = jnp.where(iota((128, 128), 0) == iota((128, 128), 1), 1.0, 0.0)
    fm0pt = nn(qm, fm0t)
    fm0 = fm0t.T
    fm0p = fm0pt.T
    fm11 = jnp.concatenate([fm1t, fm1t], axis=0).T

    mapf = [(map_ref[f] & 127).astype(f32) for f in range(6)]
    mapf = jnp.concatenate(mapf + [jnp.zeros((2, 128), f32)], axis=0)
    mapt = mmt(eye128.astype(bf16), mapf.astype(bf16))
    lanef = iota((128, 128), 1).astype(f32)

    xcopy.wait()
    for q in range(T):
        s_ref[q * 8 : q * 8 + 8, :] = x_ref[0:8, q * 128 : q * 128 + 128]
        s_ref[256 + q * 8 : 256 + q * 8 + 8, :] = x_ref[56:64, q * 128 : q * 128 + 128]
    y0 = s_ref[pl.ds(0, 32, stride=8), :]
    y1 = s_ref[pl.ds(263, 32, stride=8), :]
    f01 = jnp.concatenate([jnp.where(low32, y0, swap(y1)), jnp.where(low32, swap(y0), y1)], axis=0)
    f23 = jnp.where(low64, x_ref[:, :128], x_ref[:, 31 * 128 :])
    xh, xl = split(x_ref[...])
    f45 = mmt(jnp.concatenate([xh, xl], axis=0), sel_ref[...])
    f45 = f45[:64] + f45[64:]

    rows = []
    for pair, (left, plane) in enumerate(((fm0p, f01), (fm0, f23), (fm0, f45))):
        u = mm(left3(left), rows3(plane)) * fm11
        for half in range(2):
            keep = low if half == 0 else jnp.logical_not(low)
            val = jnp.sum(jnp.where(keep, u, 0.0), axis=1, keepdims=True)
            f = 2 * pair + half
            place = mapt[:, f : f + 1] == lanef
            rows.append(jnp.sum(jnp.where(place, val, 0.0), axis=0, keepdims=True))
    mine = jnp.concatenate(rows + [jnp.zeros((2, 128), f32)], axis=0)
    send1_ref[...] = mine
    ag_ref[me] = mine

    pl.semaphore_wait(barrier, n - 1)

    @peers
    def _(o):
        _, dev = peer(o)
        pltpu.make_async_remote_copy(src_ref=send1_ref, dst_ref=ag_ref.at[me], send_sem=ag_s, recv_sem=ag_r,
                                     device_id=dev, device_id_type=MESH).start()

    ocopy.wait()
    m0, m1, m2 = modes_ref[0], modes_ref[1], modes_ref[2]
    am_ref[0] = left3(m0)
    am_ref[1] = left3(nt(eye64, m0))
    am_ref[2] = left3(nt(nn(qm, m1), qm))
    am_ref[3] = left3(nt(nt(qm, m1), qm))
    block = (iota((128, 128), 0) >> 6) == (iota((128, 128), 1) >> 6)
    kw_ref[0] = lanes_weights(jnp.where(block, nn(nt(dupt, m2), dup), 0.0))
    kw_ref[1] = lanes_weights(jnp.where(block, nn(dupt, nn(m2, dup)), 0.0))

    @pl.loop(0, T // CH)
    def _(c):
        base = pl.multiple_of(c * (CH * 128), CH * 128)
        y = mm(am_ref[0], rows3(x_ref[:, pl.ds(base, CH * 128)]))
        stacked = jnp.concatenate([y[:, g * 128 : g * 128 + 128] for g in range(CH)], axis=0)
        s_ref[pl.ds(pl.multiple_of(c * (CH * 64), CH * 64), CH * 64), :] = lane_transform(stacked, kw_ref[0])

    wcopy.wait()
    for q in range(T):
        z_ref[q * 64 : q * 64 + 64, :] = w_ref[:, q * 128 : q * 128 + 128]

    def turned(ref, u):
        a = ref[pl.ds(u, 32, stride=64), :]
        b = ref[pl.ds(u + 32, 32, stride=64), :]
        return jnp.concatenate([jnp.where(low32, a, swap(b)), jnp.where(low32, swap(a), b)], axis=0)

    def middle(c, acc):
        fwd = jnp.concatenate([turned(s_ref, c * CH + g) for g in range(CH)], axis=1)
        wts = jnp.concatenate([turned(z_ref, c * CH + g) for g in range(CH)], axis=1)
        v = mm(am_ref[2], rows3(fwd))
        wv = wts * v
        prod = wv * v
        for g in range(CH):
            acc = acc + prod[:, g * 128 : g * 128 + 128]
        y = mm(am_ref[3], rows3(wv))
        for g in range(CH):
            p_ref[pl.ds(pl.multiple_of(64 + (c * CH + g) * 64, 64), 64), :] = y[:, g * 128 : g * 128 + 128]
        return acc

    gacc = lax.fori_loop(0, T // CH // 2, middle, jnp.zeros((64, 128), f32))

    lcopy.wait()
    cols = cols_ref[...]
    nrow = cols.shape[0]
    nz = cols.shape[1]
    wide_cols = jnp.concatenate([jnp.broadcast_to(cols[i : i + 1, :], (nz, nz)) for i in range(nrow)], axis=0)
    kk = nrow * nz
    pick_diag = iota((kk, nz), 1) == (iota((kk, nz), 0) & (nz - 1))
    colv = jnp.sum(jnp.where(pick_diag, wide_cols.astype(f32), 0.0), axis=1, keepdims=True)
    r = iota((1, n * 8), 1)
    d = r >> 3
    f = r & 7
    own = nrow * d + f
    own = jnp.where((f == 0) & (d >= ncg), nrow * (d - ncg) + 1, own)
    own = jnp.where((f == 2) & (lax.rem(d, ncg) > 0), nrow * (d - 1) + 3, own)
    own = jnp.where(f >= 6, -1, own).astype(f32)
    g1 = jnp.where(colv == own, 1.0, 0.0)
    g1 = jnp.concatenate([g1, jnp.zeros((128 - kk, n * 8), f32)], axis=0)

    g2 = g1.T.astype(bf16)
    g2 = jnp.concatenate([g2, g2], axis=1)
    g1 = g1.astype(bf16)

    pltpu.make_async_copy(ag_ref.at[pl.ds(0, n - 1)], ag_ref.at[pl.ds(0, n - 1)], ag_r).wait()
    th, tl = split(ag_ref[...].reshape(n * 8, 128))
    picked = mm(g1, th) + mm(g1, tl)
    pick_ref[...] = picked[:kk].reshape(nrow, nz, 128)
    bcopy.wait()
    spread_ref[...] = jnp.zeros_like(spread_ref)

    def coarse_row(i, acc):
        pk = pick_ref[i]
        tot = blk_ref[i, 0] * pk[0:1]
        for k in range(1, nz):
            tot = tot + blk_ref[i, k] * pk[k : k + 1]
        img = jnp.sum(tot, axis=1, keepdims=True)
        out = [jnp.sum(blk_ref[i, k] * img, axis=0, keepdims=True) for k in range(nz)]
        spread_ref[i] = jnp.concatenate(out, axis=0)
        return acc + img * img

    iacc = lax.fori_loop(0, nrow, coarse_row, jnp.zeros((128, 1), f32))
    back = mm(g2, jnp.concatenate(split(spread_ref[...].reshape(128, 128)), axis=0))
    a2s_ref[...] = back.reshape(n, 8, 128)
    a2r_ref[me] = a2s_ref[me]

    @peers
    def _(o):
        dd, dev = peer(o)
        pltpu.make_async_remote_copy(src_ref=a2s_ref.at[dd], dst_ref=a2r_ref.at[me], send_sem=a2_s, recv_sem=a2_r,
                                     device_id=dev, device_id_type=MESH).start()

    gacc = lax.fori_loop(T // CH // 2, T // CH, middle, gacc)
    gpart = jnp.sum(iacc, keepdims=True) + jnp.sum(gacc, keepdims=True)

    @pl.loop(0, T // CH)
    def _(c):
        tiles = []
        for g in range(CH):
            a = p_ref[pl.ds(64 + c * CH + g, 32, stride=64), :]
            b = p_ref[pl.ds(96 + c * CH + g, 32, stride=64), :]
            tiles.append(jnp.where(low32, a, swap(b)))
            tiles.append(jnp.where(low32, swap(a), b))
        k = lane_transform(jnp.concatenate(tiles, axis=0), kw_ref[1])
        y = jnp.concatenate([k[g * 64 : g * 64 + 64] for g in range(CH)], axis=1)
        y = mm(am_ref[1], rows3(y))
        for g in range(CH):
            s_ref[pl.ds(pl.multiple_of((c * CH + g) * 64, 64), 64), :] = y[:, g * 128 : g * 128 + 128]

    pltpu.make_async_copy(a2r_ref.at[pl.ds(0, n - 1)], a2r_ref.at[pl.ds(0, n - 1)], a2_r).wait()
    backs = jnp.sum(a2r_ref[...], axis=0)
    corr = []
    for f in range(6):
        place = mapt[:, f : f + 1] == lanef
        corr.append(jnp.sum(jnp.where(place, backs[f : f + 1], 0.0), axis=1, keepdims=True))
    e01 = mm(left3(fm0pt), rows3(jnp.where(low, corr[0], corr[1]) * fm11))
    e23 = mm(left3(fm0t), rows3(jnp.where(low, corr[2], corr[3]) * fm11))
    e45 = mm(left3(fm0t), rows3(jnp.where(low, corr[4], corr[5]) * fm11))
    eh, el = split(e45)
    eh = jnp.concatenate([eh, el], axis=0)

    @pl.loop(0, T // CH)
    def _(c):
        base = pl.multiple_of(c * (CH * 128), CH * 128)
        add = mm(eh, sel_ref[:, pl.ds(base, CH * 128)])
        for g in range(CH):
            at = pl.multiple_of((c * CH + g) * 64, 64)
            tile = add[:64, g * 128 : g * 128 + 128] + add[64:, g * 128 : g * 128 + 128]
            p_ref[pl.ds(at + 64, 64), :] = s_ref[pl.ds(at, 64), :] + tile

    p_ref[64:128, :] += jnp.where(low64, e23, 0.0)
    p_ref[T * 64 : T * 64 + 64, :] += jnp.where(low64, 0.0, e23)
    top, bottom = e01[:32], e01[32:]
    edge0 = p_ref[pl.ds(64, 32, stride=64), :] + jnp.where(low32, top, swap(bottom))
    edge1 = p_ref[pl.ds(64 + 63, 32, stride=64), :] + jnp.where(low32, swap(top), bottom)
    p_ref[pl.ds(64, 32, stride=64), :] = edge0
    p_ref[pl.ds(64 + 63, 32, stride=64), :] = edge1

    his_ref[0] = edge0
    his_ref[1] = edge1
    hjs_ref[0] = p_ref[64:128, :]
    hjs_ref[1] = p_ref[T * 64 : T * 64 + 64, :]

    sends = (
        (s > 0, s < nsub - 1, (s - 1, t), his_ref, hi_ref, 0, 1, 0),
        (s < nsub - 1, s > 0, (s + 1, t), his_ref, hi_ref, 1, 0, 1),
        (t > 0, t < ncg - 1, (s, t - 1), hjs_ref, hj_ref, 0, 1, 2),
        (t < ncg - 1, t > 0, (s, t + 1), hjs_ref, hj_ref, 1, 0, 3),
    )

    def halo(dev, src, dst, a, b, k):
        return pltpu.make_async_remote_copy(src_ref=src.at[a], dst_ref=dst.at[b], send_sem=h_s.at[k],
                                            recv_sem=h_r.at[k], device_id=dev, device_id_type=MESH)

    for does, gets, dev, src, dst, a, b, k in sends:
        @pl.when(does)
        def _():
            halo(dev, src, dst, a, b, k).start()

        @pl.when(jnp.logical_not(gets))
        def _():
            dst[b] = jnp.zeros(dst.shape[1:], f32)

    ccopy.wait()
    p_ref[0:64, :] = jnp.zeros((64, 128), f32)
    p_ref[(T + 1) * 64 : (T + 2) * 64, :] = jnp.zeros((64, 128), f32)

    row = iota((64, 128), 0)
    kpos = iota((64, 128), 1) & 63

    def stencil(q, acc):
        at = pl.multiple_of(q * 64, 64)
        x = p_ref[pl.ds(at + 64, 64), :]
        here = swap(x)
        before = swap(p_ref[pl.ds(at, 64), :])
        after = swap(p_ref[pl.ds(at + 128, 64), :])
        second = here + jnp.where(low64, before, after)
        up = jnp.where(row == 0, 0.0, pltpu.roll(x, 1, 0))
        down = jnp.where(row == 63, 0.0, pltpu.roll(x, 63, 0))
        third = jnp.where(kpos == 0, 0.0, pltpu.roll(x, 1, 1)) + jnp.where(kpos == 63, 0.0, pltpu.roll(x, 127, 1))
        cols_at = pl.ds(pl.multiple_of(q * 128, 128), 128)
        img = (cap_ref[:, cols_at] + 8.2) * x - (up + down) - 0.6 * second - 2.5 * third
        img_out[:, cols_at] = img
        p_out[:, cols_at] = x
        return acc + x * img

    cacc = lax.fori_loop(0, T, stencil, jnp.zeros((64, 128), f32), unroll=2)
    for does, gets, dev, src, dst, a, b, k in sends:
        @pl.when(gets)
        def _():
            halo(dev, src, dst, a, b, k).wait_recv()

    fix0 = 0.6 * jnp.where(low64, swap(hj_ref[0]), 0.0)
    fix1 = 0.6 * jnp.where(low64, 0.0, swap(hj_ref[1]))
    cacc = cacc - hjs_ref[0] * fix0 - hjs_ref[1] * fix1
    csum = his_ref[0] * hi_ref[0] + his_ref[1] * hi_ref[1]
    cpart = jnp.sum(cacc, axis=0, keepdims=True) - jnp.sum(csum, axis=0, keepdims=True)
    cpart = jnp.where(low, cpart + swap(cpart), gpart * (1.0 / 64.0))
    cs_ref[...] = cpart
    cr_ref[me] = cpart

    @peers
    def _(o):
        _, dev = peer(o)
        pltpu.make_async_remote_copy(src_ref=cs_ref, dst_ref=cr_ref.at[me], send_sem=c_s, recv_sem=c_r,
                                     device_id=dev, device_id_type=MESH).start()

    img_out[:, :128] = img_out[:, :128] - fix0
    img_out[:, (T - 1) * 128 :] = img_out[:, (T - 1) * 128 :] - fix1
    for q in range(T):
        at = slice(q * 128, q * 128 + 128)
        img_out[0:1, at] = img_out[0:1, at] - hi_ref[0, q : q + 1, :]
        img_out[63:64, at] = img_out[63:64, at] - hi_ref[1, q : q + 1, :]

    pltpu.make_async_copy(cr_ref.at[pl.ds(0, n - 1)], cr_ref.at[pl.ds(0, n - 1)], c_r).wait()
    both = jnp.sum(cr_ref[...], axis=0)
    curv = jnp.sum(jnp.where(low, both, 0.0), axis=1, keepdims=True)
    gamma = jnp.sum(jnp.where(low, 0.0, both), axis=1, keepdims=True)
    alpha_out[...] = gamma / curv

    pltpu.make_async_copy(ag_ref.at[pl.ds(0, n - 1)], ag_ref.at[pl.ds(0, n - 1)], ag_s).wait()
    pltpu.make_async_copy(a2r_ref.at[pl.ds(0, n - 1)], a2r_ref.at[pl.ds(0, n - 1)], a2_s).wait()
    pltpu.make_async_copy(cr_ref.at[pl.ds(0, n - 1)], cr_ref.at[pl.ds(0, n - 1)], c_s).wait()
    for does, gets, dev, src, dst, a, b, k in sends:
        @pl.when(does)
        def _():
            halo(dev, src, dst, a, b, k).wait_send()


def body(nsub, ncg, source, capacity, fd_weights, fd_modes, face_modes, coarse_map, fsai_cols, fsai_blocks):
    n = nsub * ncg
    nrow, nz = fsai_cols.shape
    vm = pl.BlockSpec(memory_space=pltpu.VMEM)
    hbm = pl.BlockSpec(memory_space=pltpu.HBM)
    field = jax.ShapeDtypeStruct(source.shape, f32)
    V = pltpu.VMEM
    dma = pltpu.SemaphoreType.DMA
    p, img, alpha = pl.pallas_call(
        functools.partial(kernel, nsub, ncg),
        out_shape=(field, field, jax.ShapeDtypeStruct((1, 1), f32)),
        in_specs=[hbm] * 8,
        out_specs=(vm, vm, vm),
        scratch_shapes=[
            V(source.shape, f32),
            V(fd_modes.shape, f32),
            V((2, 64, 128), f32),
            V((6, 1, 128), jnp.int32),
            V(fsai_cols.shape, jnp.int32),
            V((T * 64, 128), f32),
            V((T * 64, 128), f32),
            V((64, T * 128), f32),
            V(((T + 2) * 64, 128), f32),
            V((64, T * 128), f32),
            V(fsai_blocks.shape, f32),
            V((128, T * 128), bf16),
            V((4, 64, 192), bf16),
            V((2, 256, 256), bf16),
            V((n, 8, 128), f32),
            V((8, 128), f32),
            V((n, 8, 128), f32),
            V((n, 8, 128), f32),
            V((nrow, nz, 128), f32),
            V((128 // nz, nz, 128), f32),
            V((2, 32, 128), f32),
            V((2, 32, 128), f32),
            V((2, 64, 128), f32),
            V((2, 64, 128), f32),
            V((1, 128), f32),
            V((n, 1, 128), f32),
            dma((8,)),
            dma, dma, dma, dma,
            dma((4,)), dma((4,)),
            dma, dma,
        ],
        compiler_params=pltpu.CompilerParams(collective_id=0, has_side_effects=True,
                                             vmem_limit_bytes=48 * 1024 * 1024),
        cost_estimate=pl.CostEstimate(flops=10**9, bytes_accessed=8 * 2**20, transcendentals=0),
        name="step",
    )(*(pltpu.with_memory_space_constraint(v, pltpu.HBM) for v in (
        source, fd_modes, jnp.swapaxes(face_modes, 1, 2), coarse_map.reshape(-1, 1, coarse_map.shape[-1]),
        fsai_cols, capacity, fd_weights, fsai_blocks)))
    a = alpha[0, 0]
    return a * p, source - a * img


def solution(mesh):
    in_specs = (
        P("sub", "cgrp"),
        P("sub", "cgrp"),
        P("sub", "cgrp"),
        P(),
        P(),
        P("sub", "cgrp", None, None),
        P(("sub", "cgrp"), None),
        P(("sub", "cgrp"), None, None, None),
    )
    out_specs = (P("sub", "cgrp"), P("sub", "cgrp"))
    step = functools.partial(body, mesh.shape["sub"], mesh.shape["cgrp"])
    return jax.shard_map(step, mesh=mesh, in_specs=in_specs, out_specs=out_specs, check_vma=False)
```

profile of v0, /device:TPU:0, one launch (start us, length us, event | category | flops | bytes accessed | tf_op | source)
XLA Modules:
  0.0 30.6 jit_solution(10050003567044812864)
XLA Ops:
  0.6 0.0 copy-start
  0.6 27.8 %step.1 = (f32[64,4096]{1,0:T(8,128)S(1)}, f32[64,4096]{1,0:T(8,128)S(1)}, f32[1,1]{1,0:T(1,128)}) custom-call(f32[64,4096]{1,0:T(8,128)} %x_any.1, f32[3,64,64]{2,1,0:T(8,128)} %modes_any.1, f32[2,64,128]{2,1,0:T(8,128)} %bitcast.3, s32[6,1,128]{2,1,0:T(1,128)} %bitcast.4, s32[6,8]{1,0:T(8,128)} %cols_any.1, f32[64,4096]{1,0:T(8,128)} %cap_any.1, ...), custom_call_target="tpu_custom_call" | custom-call | flops 1000000000 | bytes 8388608 | tf_op jit(solution)/shard_map/step/pallas_call | solution.py:409
  28.4 0.0 copy-done
  28.4 2.2 %multiply_subtract_fusion = (f32[64,4096]{1,0:T(8,128)}, f32[64,4096]{1,0:T(8,128)}) fusion(f32[64,4096]{1,0:T(8,128)S(1)} %copy-done, f32[64,4096]{1,0:T(8,128)S(1)} %get-tuple-element.7, f32[]{:T(128)} %bitcast.2, f32[64,4096]{1,0:T(8,128)S(1)} %get-tuple-element.6), kind=kLoop, calls=%fused_computation | loop fusion | flops 786432 | bytes 5242884 | tf_op jit(solution)/shard_map/sub | solution.py:454
Async XLA Ops:
  0.6 27.8 %copy-start = (f32[64,4096]{1,0:T(8,128)S(1)}, f32[64,4096]{1,0:T(8,128)}, u32[]{:S(2)}) copy-start(f32[64,4096]{1,0:T(8,128)} %x_any.1) | copy-start | bytes 3145732
where the time goes:
time: 30.7 us; the launch traced here: 30.6 us
  Pallas kernels  27.8 us (91%)
  other arithmetic  2.17 us (7%)
  between operations  0.66 us (2%)
    pallas_call x1, Pallas kernels, body(): pl.pallas_call(functools.partial(kernel, nsub, ncg), out_shape=(field, fi...  27.8 us
    sub x1, other arithmetic, body(): return (a * p, source - a * img)  2.17 us

commit v1 on v0

--- a/solution.py
+++ b/solution.py
@@ -87,13 +87,30 @@
         early[-1].start()
     fcopy, mcopy, xcopy, ocopy, lcopy, wcopy, bcopy, ccopy = early
 
+    def mirror(v, bits):
+        out = v
+        for k in range(8):
+            if bits >> k & 1:
+                out = out + (1 << k) - (2 << k) * lax.rem(lax.div(v, 1 << k), 2)
+        return out
+
     def peers(step):
         if n > 32:
-            pl.loop(1, n)(step)
+            @pl.loop(1, n)
+            def _(o):
+                step(*peer(o))
         else:
-            for o in range(1, n):
-                step(o)
-
+            pairs = [(a, b) for a in range(nsub) for b in range(ncg) if a or b]
+            for a, b in sorted(pairs, key=lambda ab: -(ab[0] + (ab[1] >> 1 & 1) + (ab[1] >> 2 & 1))):
+                ds, dt = mirror(s, a), mirror(t, b)
+                step(ds * ncg + dt, (ds, dt))
+
+    def arrived(ref, rows, sem):
+        part = ref.at[pl.ds(0, n - 1), pl.ds(0, rows)]
+        pltpu.make_async_copy(part, part, sem).wait()
+
+    ag_ref[...] = jnp.zeros_like(ag_ref)
+    a2r_ref[...] = jnp.zeros_like(a2r_ref)
     barrier = pltpu.get_barrier_semaphore()
 
     @pl.loop(1, n)
@@ -165,9 +182,9 @@
     pl.semaphore_wait(barrier, n - 1)
 
     @peers
-    def _(o):
-        _, dev = peer(o)
-        pltpu.make_async_remote_copy(src_ref=send1_ref, dst_ref=ag_ref.at[me], send_sem=ag_s, recv_sem=ag_r,
+    def _(dd, dev):
+        pltpu.make_async_remote_copy(src_ref=send1_ref.at[pl.ds(0, 6)], dst_ref=ag_ref.at[me, pl.ds(0, 6)],
+                                     send_sem=ag_s, recv_sem=ag_r,
                                      device_id=dev, device_id_type=MESH).start()
 
     ocopy.wait()
@@ -233,7 +250,7 @@
     g2 = jnp.concatenate([g2, g2], axis=1)
     g1 = g1.astype(bf16)
 
-    pltpu.make_async_copy(ag_ref.at[pl.ds(0, n - 1)], ag_ref.at[pl.ds(0, n - 1)], ag_r).wait()
+    arrived(ag_ref, 6, ag_r)
     th, tl = split(ag_ref[...].reshape(n * 8, 128))
     picked = mm(g1, th) + mm(g1, tl)
     pick_ref[...] = picked[:kk].reshape(nrow, nz, 128)
@@ -256,9 +273,9 @@
     a2r_ref[me] = a2s_ref[me]
 
     @peers
-    def _(o):
-        dd, dev = peer(o)
-        pltpu.make_async_remote_copy(src_ref=a2s_ref.at[dd], dst_ref=a2r_ref.at[me], send_sem=a2_s, recv_sem=a2_r,
+    def _(dd, dev):
+        pltpu.make_async_remote_copy(src_ref=a2s_ref.at[dd, pl.ds(0, 6)], dst_ref=a2r_ref.at[me, pl.ds(0, 6)],
+                                     send_sem=a2_s, recv_sem=a2_r,
                                      device_id=dev, device_id_type=MESH).start()
 
     gacc = lax.fori_loop(T // CH // 2, T // CH, middle, gacc)
@@ -278,7 +295,7 @@
         for g in range(CH):
             s_ref[pl.ds(pl.multiple_of((c * CH + g) * 64, 64), 64), :] = y[:, g * 128 : g * 128 + 128]
 
-    pltpu.make_async_copy(a2r_ref.at[pl.ds(0, n - 1)], a2r_ref.at[pl.ds(0, n - 1)], a2_r).wait()
+    arrived(a2r_ref, 6, a2_r)
     backs = jnp.sum(a2r_ref[...], axis=0)
     corr = []
     for f in range(6):
@@ -371,8 +388,7 @@
     cr_ref[me] = cpart
 
     @peers
-    def _(o):
-        _, dev = peer(o)
+    def _(dd, dev):
         pltpu.make_async_remote_copy(src_ref=cs_ref, dst_ref=cr_ref.at[me], send_sem=c_s, recv_sem=c_r,
                                      device_id=dev, device_id_type=MESH).start()
 
@@ -389,8 +405,8 @@
     gamma = jnp.sum(jnp.where(low, 0.0, both), axis=1, keepdims=True)
     alpha_out[...] = gamma / curv
 
-    pltpu.make_async_copy(ag_ref.at[pl.ds(0, n - 1)], ag_ref.at[pl.ds(0, n - 1)], ag_s).wait()
-    pltpu.make_async_copy(a2r_ref.at[pl.ds(0, n - 1)], a2r_ref.at[pl.ds(0, n - 1)], a2_s).wait()
+    arrived(ag_ref, 6, ag_s)
+    arrived(a2r_ref, 6, a2_s)
     pltpu.make_async_copy(cr_ref.at[pl.ds(0, n - 1)], cr_ref.at[pl.ds(0, n - 1)], c_s).wait()
     for does, gets, dev, src, dst, a, b, k in sends:
         @pl.when(does)

time: 30.7 us -> 29 us (0.945)
  Pallas kernels: 27.8 us -> 26 us
    pallas_call x1, Pallas kernels: 27.8 us -> 26 us  [body(): pl.pallas_call(functools.partial(kernel, nsub, ncg), out_shape=(field, fi...]
where the time goes in v1:
time: 29 us; the launch traced here: 28.9 us
  Pallas kernels  26 us (90%)
  other arithmetic  2.17 us (7%)
  between operations  0.66 us (2%)
    pallas_call x1, Pallas kernels, body(): pl.pallas_call(functools.partial(kernel, nsub, ncg), out_shape=(field, fi...  26 us
    sub x1, other arithmetic, body(): return (a * p, source - a * img)  2.17 us

profile of v1, /device:TPU:0, one launch (start us, length us, event | category | flops | bytes accessed | tf_op | source)
XLA Modules:
  0.0 28.9 jit_solution(3409169629039729980)
XLA Ops:
  0.6 0.0 copy-start
  0.6 26.0 %step.1 = (f32[64,4096]{1,0:T(8,128)S(1)}, f32[64,4096]{1,0:T(8,128)S(1)}, f32[1,1]{1,0:T(1,128)}) custom-call(f32[64,4096]{1,0:T(8,128)} %x_any.1, f32[3,64,64]{2,1,0:T(8,128)} %modes_any.1, f32[2,64,128]{2,1,0:T(8,128)} %bitcast.3, s32[6,1,128]{2,1,0:T(1,128)} %bitcast.4, s32[6,8]{1,0:T(8,128)} %cols_any.1, f32[64,4096]{1,0:T(8,128)} %cap_any.1, ...), custom_call_target="tpu_custom_call" | custom-call | flops 1000000000 | bytes 8388608 | tf_op jit(solution)/shard_map/step/pallas_call | solution.py:425
  26.7 0.0 copy-done
  26.7 2.2 %multiply_subtract_fusion = (f32[64,4096]{1,0:T(8,128)}, f32[64,4096]{1,0:T(8,128)}) fusion(f32[64,4096]{1,0:T(8,128)S(1)} %copy-done, f32[64,4096]{1,0:T(8,128)S(1)} %get-tuple-element.7, f32[]{:T(128)} %bitcast.2, f32[64,4096]{1,0:T(8,128)S(1)} %get-tuple-element.6), kind=kLoop, calls=%fused_computation | loop fusion | flops 786432 | bytes 5242884 | tf_op jit(solution)/shard_map/sub | solution.py:470
Async XLA Ops:
  0.6 26.1 %copy-start = (f32[64,4096]{1,0:T(8,128)S(1)}, f32[64,4096]{1,0:T(8,128)}, u32[]{:S(2)}) copy-start(f32[64,4096]{1,0:T(8,128)} %x_any.1) | copy-start | bytes 3145732

commit v2 on v1

--- a/solution.py
+++ b/solution.py
@@ -64,8 +64,8 @@
 
 
 def kernel(nsub, ncg, x_any, modes_any, face_any, map_any, cols_any, cap_any, wt_any, blk_any,
-           p_out, img_out, alpha_out,
-           x_ref, modes_ref, face_ref, map_ref, cols_ref,
+           p_out, img_out, x_ref, alpha_out,
+           modes_ref, face_ref, map_ref, cols_ref,
            s_ref, z_ref, w_ref, p_ref, cap_ref, blk_ref, sel_ref, am_ref, kw_ref,
            ag_ref, send1_ref, a2s_ref, a2r_ref, pick_ref, spread_ref,
            hi_ref, his_ref, hj_ref, hjs_ref, cs_ref, cr_ref,
@@ -79,13 +79,12 @@
         d = lax.rem(me + o, n)
         return d, (lax.div(d, ncg), lax.rem(d, ncg))
 
-    early = []
-    for k, (src, dst) in enumerate(((face_any, face_ref), (map_any, map_ref), (x_any, x_ref),
-                                    (modes_any, modes_ref), (cols_any, cols_ref),
-                                    (wt_any, w_ref), (blk_any, blk_ref), (cap_any, cap_ref))):
-        early.append(pltpu.make_async_copy(src, dst, dsem.at[k]))
-        early[-1].start()
-    fcopy, mcopy, xcopy, ocopy, lcopy, wcopy, bcopy, ccopy = early
+    early = [pltpu.make_async_copy(src, dst, dsem.at[k]) for k, (src, dst) in enumerate((
+        (x_any, x_ref), (face_any, face_ref), (map_any, map_ref), (modes_any, modes_ref), (cols_any, cols_ref),
+        (wt_any, w_ref), (blk_any, blk_ref), (cap_any, cap_ref)))]
+    for copy in early[:5]:
+        copy.start()
+    xcopy, fcopy, mcopy, ocopy, lcopy, wcopy, bcopy, ccopy = early
 
     def mirror(v, bits):
         out = v
@@ -155,6 +154,8 @@
     lanef = iota((128, 128), 1).astype(f32)
 
     xcopy.wait()
+    for copy in early[5:]:
+        copy.start()
     for q in range(T):
         s_ref[q * 8 : q * 8 + 8, :] = x_ref[0:8, q * 128 : q * 128 + 128]
         s_ref[256 + q * 8 : 256 + q * 8 + 8, :] = x_ref[56:64, q * 128 : q * 128 + 128]
@@ -197,12 +198,11 @@
     kw_ref[0] = lanes_weights(jnp.where(block, nn(nt(dupt, m2), dup), 0.0))
     kw_ref[1] = lanes_weights(jnp.where(block, nn(dupt, nn(m2, dup)), 0.0))
 
-    @pl.loop(0, T // CH)
-    def _(c):
-        base = pl.multiple_of(c * (CH * 128), CH * 128)
+    for c in range(T // CH):
+        base = (c * (CH * 128))
         y = mm(am_ref[0], rows3(x_ref[:, pl.ds(base, CH * 128)]))
         stacked = jnp.concatenate([y[:, g * 128 : g * 128 + 128] for g in range(CH)], axis=0)
-        s_ref[pl.ds(pl.multiple_of(c * (CH * 64), CH * 64), CH * 64), :] = lane_transform(stacked, kw_ref[0])
+        s_ref[pl.ds((c * (CH * 64)), CH * 64), :] = lane_transform(stacked, kw_ref[0])
 
     wcopy.wait()
     for q in range(T):
@@ -223,10 +223,12 @@
             acc = acc + prod[:, g * 128 : g * 128 + 128]
         y = mm(am_ref[3], rows3(wv))
         for g in range(CH):
-            p_ref[pl.ds(pl.multiple_of(64 + (c * CH + g) * 64, 64), 64), :] = y[:, g * 128 : g * 128 + 128]
+            p_ref[pl.ds((64 + (c * CH + g) * 64), 64), :] = y[:, g * 128 : g * 128 + 128]
         return acc
 
-    gacc = lax.fori_loop(0, T // CH // 2, middle, jnp.zeros((64, 128), f32))
+    gacc = jnp.zeros((64, 128), f32)
+    for c in range(T // CH // 2):
+        gacc = middle(c, gacc)
 
     lcopy.wait()
     cols = cols_ref[...]
@@ -278,11 +280,11 @@
                                      send_sem=a2_s, recv_sem=a2_r,
                                      device_id=dev, device_id_type=MESH).start()
 
-    gacc = lax.fori_loop(T // CH // 2, T // CH, middle, gacc)
+    for c in range(T // CH // 2, T // CH):
+        gacc = middle(c, gacc)
     gpart = jnp.sum(iacc, keepdims=True) + jnp.sum(gacc, keepdims=True)
 
-    @pl.loop(0, T // CH)
-    def _(c):
+    for c in range(T // CH):
         tiles = []
         for g in range(CH):
             a = p_ref[pl.ds(64 + c * CH + g, 32, stride=64), :]
@@ -293,7 +295,7 @@
         y = jnp.concatenate([k[g * 64 : g * 64 + 64] for g in range(CH)], axis=1)
         y = mm(am_ref[1], rows3(y))
         for g in range(CH):
-            s_ref[pl.ds(pl.multiple_of((c * CH + g) * 64, 64), 64), :] = y[:, g * 128 : g * 128 + 128]
+            s_ref[pl.ds(((c * CH + g) * 64), 64), :] = y[:, g * 128 : g * 128 + 128]
 
     arrived(a2r_ref, 6, a2_r)
     backs = jnp.sum(a2r_ref[...], axis=0)
@@ -307,12 +309,11 @@
     eh, el = split(e45)
     eh = jnp.concatenate([eh, el], axis=0)
 
-    @pl.loop(0, T // CH)
-    def _(c):
-        base = pl.multiple_of(c * (CH * 128), CH * 128)
+    for c in range(T // CH):
+        base = (c * (CH * 128))
         add = mm(eh, sel_ref[:, pl.ds(base, CH * 128)])
         for g in range(CH):
-            at = pl.multiple_of((c * CH + g) * 64, 64)
+            at = ((c * CH + g) * 64)
             tile = add[:64, g * 128 : g * 128 + 128] + add[64:, g * 128 : g * 128 + 128]
             p_ref[pl.ds(at + 64, 64), :] = s_ref[pl.ds(at, 64), :] + tile
 
@@ -359,10 +360,7 @@
     def stencil(q, acc):
         at = pl.multiple_of(q * 64, 64)
         x = p_ref[pl.ds(at + 64, 64), :]
-        here = swap(x)
-        before = swap(p_ref[pl.ds(at, 64), :])
-        after = swap(p_ref[pl.ds(at + 128, 64), :])
-        second = here + jnp.where(low64, before, after)
+        second = swap(x + jnp.where(low64, p_ref[pl.ds(at + 128, 64), :], p_ref[pl.ds(at, 64), :]))
         up = jnp.where(row == 0, 0.0, pltpu.roll(x, 1, 0))
         down = jnp.where(row == 63, 0.0, pltpu.roll(x, 63, 0))
         third = jnp.where(kpos == 0, 0.0, pltpu.roll(x, 1, 1)) + jnp.where(kpos == 63, 0.0, pltpu.roll(x, 127, 1))
@@ -372,7 +370,7 @@
         p_out[:, cols_at] = x
         return acc + x * img
 
-    cacc = lax.fori_loop(0, T, stencil, jnp.zeros((64, 128), f32), unroll=2)
+    cacc = lax.fori_loop(0, T, stencil, jnp.zeros((64, 128), f32), unroll=4)
     for does, gets, dev, src, dst, a, b, k in sends:
         @pl.when(gets)
         def _():
@@ -414,6 +412,21 @@
             halo(dev, src, dst, a, b, k).wait_send()
 
 
+def finish(p_ref, img_ref, x_ref, alpha_ref, sol_any, res_any, sol_ref, res_ref, sem):
+    copies = []
+    a = alpha_ref[...]
+    for c in range(8):
+        at = pl.ds(c * 8, 8)
+        sol_ref[at, :] = a * p_ref[at, :]
+        copies.append(pltpu.make_async_copy(sol_ref.at[at], sol_any.at[at], sem.at[0, c]))
+        copies[-1].start()
+        res_ref[at, :] = x_ref[at, :] - a * img_ref[at, :]
+        copies.append(pltpu.make_async_copy(res_ref.at[at], res_any.at[at], sem.at[1, c]))
+        copies[-1].start()
+    for copy in copies:
+        copy.wait()
+
+
 def body(nsub, ncg, source, capacity, fd_weights, fd_modes, face_modes, coarse_map, fsai_cols, fsai_blocks):
     n = nsub * ncg
     nrow, nz = fsai_cols.shape
@@ -422,13 +435,12 @@
     field = jax.ShapeDtypeStruct(source.shape, f32)
     V = pltpu.VMEM
     dma = pltpu.SemaphoreType.DMA
-    p, img, alpha = pl.pallas_call(
+    p, img, x, alpha = pl.pallas_call(
         functools.partial(kernel, nsub, ncg),
-        out_shape=(field, field, jax.ShapeDtypeStruct((1, 1), f32)),
+        out_shape=(field, field, field, jax.ShapeDtypeStruct((1, 1), f32)),
         in_specs=[hbm] * 8,
-        out_specs=(vm, vm, vm),
+        out_specs=(vm, vm, vm, vm),
         scratch_shapes=[
-            V(source.shape, f32),
             V(fd_modes.shape, f32),
             V((2, 64, 128), f32),
             V((6, 1, 128), jnp.int32),
@@ -466,8 +478,15 @@
     )(*(pltpu.with_memory_space_constraint(v, pltpu.HBM) for v in (
         source, fd_modes, jnp.swapaxes(face_modes, 1, 2), coarse_map.reshape(-1, 1, coarse_map.shape[-1]),
         fsai_cols, capacity, fd_weights, fsai_blocks)))
-    a = alpha[0, 0]
-    return a * p, source - a * img
+    return pl.pallas_call(
+        finish,
+        out_shape=(field, field),
+        in_specs=[vm] * 4,
+        out_specs=(hbm, hbm),
+        scratch_shapes=[V(source.shape, f32), V(source.shape, f32), dma((2, 8))],
+        cost_estimate=pl.CostEstimate(flops=2**20, bytes_accessed=2 * 2**20, transcendentals=0),
+        name="finish",
+    )(*(pltpu.with_memory_space_constraint(v, pltpu.VMEM) for v in (p, img, x, alpha)))
 
 
 def solution(mesh):

time: 29 us -> 28.3 us (0.976)
  other arithmetic: 2.17 us -> 0 us
  Pallas kernels: 26 us -> 27.5 us
    sub x1 -> x0, other arithmetic: 2.17 us -> none  [body(): return (a * p, source - a * img)]
    pallas_call x0 -> x1, Pallas kernels: none -> 2.08 us  [body(): pl.pallas_call(finish, out_shape=(field, field), in_specs=[vm] * 4, out_s...]
    pallas_call x1, Pallas kernels: 26 us -> 25.4 us  [body(): pl.pallas_call(functools.partial(kernel, nsub, ncg), out_shape=(field, fi...]
where the time goes in v2:
time: 28.3 us; the launch traced here: 28.2 us
  Pallas kernels  27.5 us (97%)
  between operations  0.64 us (2%)
    pallas_call x1, Pallas kernels, body(): pl.pallas_call(functools.partial(kernel, nsub, ncg), out_shape=(field, fi...  25.4 us
    pallas_call x1, Pallas kernels, body(): pl.pallas_call(finish, out_shape=(field, field), in_specs=[vm] * 4, out_s...  2.08 us

profile of v2, /device:TPU:0, one launch (start us, length us, event | category | flops | bytes accessed | tf_op | source)
XLA Modules:
  0.0 28.2 jit_solution(1716171755131434471)
XLA Ops:
  0.6 25.4 %step.1 = (f32[64,4096]{1,0:T(8,128)S(1)}, f32[64,4096]{1,0:T(8,128)S(1)}, f32[64,4096]{1,0:T(8,128)S(1)}, f32[1,1]{1,0:T(1,128)}) custom-call(f32[64,4096]{1,0:T(8,128)} %x_any.1, f32[3,64,64]{2,1,0:T(8,128)} %modes_any.1, f32[2,64,128]{2,1,0:T(8,128)} %bitcast.2, s32[6,1,128]{2,1,0:T(1,128)} %bitcast.3, s32[6,8]{1,0:T(8,128)} %cols_any.1, ...), custom_call_target="tpu_custom_call" | custom-call | flops 1000000000 | bytes 8388608 | tf_op jit(solution)/shard_map/step/pallas_call | solution.py:438
  26.1 2.1 %finish.1 = (f32[64,4096]{1,0:T(8,128)}, f32[64,4096]{1,0:T(8,128)}) custom-call(f32[64,4096]{1,0:T(8,128)S(1)} %get-tuple-element.6.p_ref, f32[64,4096]{1,0:T(8,128)S(1)} %get-tuple-element.7.img_ref, f32[64,4096]{1,0:T(8,128)S(1)} %get-tuple-element.8.x_ref, f32[1,1]{1,0:T(1,128)} %get-tuple-element.9.alpha_ref), custom_call_target="tpu_custom_call" | custom-call | flops 1048576 | bytes 2097152 | tf_op jit(solution)/shard_map/finish/pallas_call | solution.py:481

commit v3 on v2

--- a/solution.py
+++ b/solution.py
@@ -68,7 +68,7 @@
            modes_ref, face_ref, map_ref, cols_ref,
            s_ref, z_ref, w_ref, p_ref, cap_ref, blk_ref, sel_ref, am_ref, kw_ref,
            ag_ref, send1_ref, a2s_ref, a2r_ref, pick_ref, spread_ref,
-           hi_ref, his_ref, hj_ref, hjs_ref, cs_ref, cr_ref,
+           hi_ref, his_ref, hj_ref, hjs_ref, cs_ref, cr_ref, l_ref, strip_ref,
            dsem, ag_s, ag_r, a2_s, a2_r, h_s, h_r, c_s, c_r):
     n = nsub * ncg
     s = lax.axis_index("sub")
@@ -156,26 +156,33 @@
     xcopy.wait()
     for copy in early[5:]:
         copy.start()
-    for q in range(T):
-        s_ref[q * 8 : q * 8 + 8, :] = x_ref[0:8, q * 128 : q * 128 + 128]
-        s_ref[256 + q * 8 : 256 + q * 8 + 8, :] = x_ref[56:64, q * 128 : q * 128 + 128]
-    y0 = s_ref[pl.ds(0, 32, stride=8), :]
-    y1 = s_ref[pl.ds(263, 32, stride=8), :]
-    f01 = jnp.concatenate([jnp.where(low32, y0, swap(y1)), jnp.where(low32, swap(y0), y1)], axis=0)
-    f23 = jnp.where(low64, x_ref[:, :128], x_ref[:, 31 * 128 :])
-    xh, xl = split(x_ref[...])
-    f45 = mmt(jnp.concatenate([xh, xl], axis=0), sel_ref[...])
-    f45 = f45[:64] + f45[64:]
+
+    def pair(a, b):
+        return jnp.concatenate([jnp.where(low32, a, swap(b)), jnp.where(low32, swap(a), b)], axis=0)
+
+    def planes(ref):
+        for q in range(T):
+            strip_ref[q * 8 : q * 8 + 8, :] = ref[0:8, q * 128 : q * 128 + 128]
+            strip_ref[256 + q * 8 : 256 + q * 8 + 8, :] = ref[56:64, q * 128 : q * 128 + 128]
+        y0 = strip_ref[pl.ds(0, 32, stride=8), :]
+        y1 = strip_ref[pl.ds(263, 32, stride=8), :]
+        f01 = pair(y0, y1)
+        f23 = jnp.where(low64, ref[:, :128], ref[:, 31 * 128 :])
+        f45 = mmt(jnp.concatenate(split(ref[...]), axis=0), sel_ref[...])
+        return f01, f23, f45[:64] + f45[64:]
+
+    def restrict(f01, f23, f45):
+        vals = []
+        for left, plane in ((fm0p, f01), (fm0, f23), (fm0, f45)):
+            u = mm(left3(left), rows3(plane)) * fm11
+            vals.append(jnp.sum(jnp.where(low, u, 0.0), axis=1, keepdims=True))
+            vals.append(jnp.sum(jnp.where(low, 0.0, u), axis=1, keepdims=True))
+        return vals
 
     rows = []
-    for pair, (left, plane) in enumerate(((fm0p, f01), (fm0, f23), (fm0, f45))):
-        u = mm(left3(left), rows3(plane)) * fm11
-        for half in range(2):
-            keep = low if half == 0 else jnp.logical_not(low)
-            val = jnp.sum(jnp.where(keep, u, 0.0), axis=1, keepdims=True)
-            f = 2 * pair + half
-            place = mapt[:, f : f + 1] == lanef
-            rows.append(jnp.sum(jnp.where(place, val, 0.0), axis=0, keepdims=True))
+    for f, val in enumerate(restrict(*planes(x_ref))):
+        place = mapt[:, f : f + 1] == lanef
+        rows.append(jnp.sum(jnp.where(place, val, 0.0), axis=0, keepdims=True))
     mine = jnp.concatenate(rows + [jnp.zeros((2, 128), f32)], axis=0)
     send1_ref[...] = mine
     ag_ref[me] = mine
@@ -227,8 +234,11 @@
         return acc
 
     gacc = jnp.zeros((64, 128), f32)
-    for c in range(T // CH // 2):
+    for c in range(T // CH):
         gacc = middle(c, gacc)
+
+    ccopy.wait()
+    cap01, cap23, cap45 = planes(cap_ref)
 
     lcopy.wait()
     cols = cols_ref[...]
@@ -269,7 +279,9 @@
         spread_ref[i] = jnp.concatenate(out, axis=0)
         return acc + img * img
 
-    iacc = lax.fori_loop(0, nrow, coarse_row, jnp.zeros((128, 1), f32))
+    iacc = jnp.zeros((128, 1), f32)
+    for i in range(nrow):
+        iacc = coarse_row(i, iacc)
     back = mm(g2, jnp.concatenate(split(spread_ref[...].reshape(128, 128)), axis=0))
     a2s_ref[...] = back.reshape(n, 8, 128)
     a2r_ref[me] = a2s_ref[me]
@@ -280,8 +292,6 @@
                                      send_sem=a2_s, recv_sem=a2_r,
                                      device_id=dev, device_id_type=MESH).start()
 
-    for c in range(T // CH // 2, T // CH):
-        gacc = middle(c, gacc)
     gpart = jnp.sum(iacc, keepdims=True) + jnp.sum(gacc, keepdims=True)
 
     for c in range(T // CH):
@@ -295,7 +305,77 @@
         y = jnp.concatenate([k[g * 64 : g * 64 + 64] for g in range(CH)], axis=1)
         y = mm(am_ref[1], rows3(y))
         for g in range(CH):
-            s_ref[pl.ds(((c * CH + g) * 64), 64), :] = y[:, g * 128 : g * 128 + 128]
+            l_ref[pl.ds(((c * CH + g) * 64 + 64), 64), :] = y[:, g * 128 : g * 128 + 128]
+
+    row = iota((64, 128), 0)
+    kpos = iota((64, 128), 1) & 63
+
+    def operate(ref, q):
+        at = q * 64
+        x = ref[pl.ds(at + 64, 64), :]
+        second = swap(x + jnp.where(low64, ref[pl.ds(at + 128, 64), :], ref[pl.ds(at, 64), :]))
+        up = jnp.where(row == 0, 0.0, pltpu.roll(x, 1, 0))
+        down = jnp.where(row == 63, 0.0, pltpu.roll(x, 63, 0))
+        third = jnp.where(kpos == 0, 0.0, pltpu.roll(x, 1, 1)) + jnp.where(kpos == 63, 0.0, pltpu.roll(x, 127, 1))
+        cols_at = pl.ds(q * 128, 128)
+        img = (cap_ref[:, cols_at] + 8.2) * x - (up + down) - 0.6 * second - 2.5 * third
+        img_out[:, cols_at] = img
+        return x, img
+
+    sends = (
+        (s > 0, s < nsub - 1, (s - 1, t), his_ref, hi_ref, 0, 1, 0),
+        (s < nsub - 1, s > 0, (s + 1, t), his_ref, hi_ref, 1, 0, 1),
+        (t > 0, t < ncg - 1, (s, t - 1), hjs_ref, hj_ref, 0, 1, 2),
+        (t < ncg - 1, t > 0, (s, t + 1), hjs_ref, hj_ref, 1, 0, 3),
+    )
+
+    def halo(turn, dev, src, dst, a, b, k):
+        return pltpu.make_async_remote_copy(src_ref=src.at[turn, a], dst_ref=dst.at[turn, b], send_sem=h_s.at[turn, k],
+                                            recv_sem=h_r.at[turn, k], device_id=dev, device_id_type=MESH)
+
+    def send_halo(turn, edge0, edge1, ref):
+        his_ref[turn, 0] = edge0
+        his_ref[turn, 1] = edge1
+        hjs_ref[turn, 0] = jnp.where(low32, ref[64:96, :], swap(ref[96:128, :]))
+        hjs_ref[turn, 1] = jnp.where(low32, swap(ref[T * 64 : T * 64 + 32, :]), ref[T * 64 + 32 : T * 64 + 64, :])
+        for does, gets, dev, src, dst, a, b, k in sends:
+            @pl.when(does)
+            def _():
+                halo(turn, dev, src, dst, a, b, k).start()
+
+            @pl.when(jnp.logical_not(gets))
+            def _():
+                dst[turn, b] = jnp.zeros(dst.shape[2:], f32)
+
+    def await_halo(turn):
+        for does, gets, dev, src, dst, a, b, k in sends:
+            @pl.when(gets)
+            def _():
+                halo(turn, dev, src, dst, a, b, k).wait_recv()
+
+    l_ref[0:64, :] = jnp.zeros((64, 128), f32)
+    l_ref[(T + 1) * 64 : (T + 2) * 64, :] = jnp.zeros((64, 128), f32)
+    ledge0 = l_ref[pl.ds(64, 32, stride=64), :]
+    ledge1 = l_ref[pl.ds(64 + 63, 32, stride=64), :]
+    send_halo(0, ledge0, ledge1, l_ref)
+    cacc = jnp.zeros((64, 128), f32)
+    for q in range(T):
+        value, img = operate(l_ref, q)
+        cacc = cacc + value * img
+    l01 = pair(ledge0, ledge1)
+    l23 = jnp.where(low64, l_ref[64:128, :], l_ref[T * 64 : T * 64 + 64, :])
+    image_vals = restrict(*planes(img_out))
+
+    fm00 = jnp.concatenate([fm0t, fm0t], axis=0).T
+    fm0p3, fm03, fm13, fm1p3 = left3(fm0pt), left3(fm0t), left3(fm1t), left3(nn(qm, fm1t))
+    inner_row = (row > 0) & (row < 63)
+    inner_col = (kpos > 0) & (kpos < 63)
+    last_row = row == 63
+    last_col = kpos == 63
+    s_low = jnp.where(s > 0, 1.0, 0.0)
+    s_high = jnp.where(s < nsub - 1, 1.0, 0.0)
+    t_low = jnp.where(t > 0, 0.6, 0.0)
+    t_high = jnp.where(t < ncg - 1, 0.6, 0.0)
 
     arrived(a2r_ref, 6, a2_r)
     backs = jnp.sum(a2r_ref[...], axis=0)
@@ -303,9 +383,64 @@
     for f in range(6):
         place = mapt[:, f : f + 1] == lanef
         corr.append(jnp.sum(jnp.where(place, backs[f : f + 1], 0.0), axis=1, keepdims=True))
-    e01 = mm(left3(fm0pt), rows3(jnp.where(low, corr[0], corr[1]) * fm11))
-    e23 = mm(left3(fm0t), rows3(jnp.where(low, corr[2], corr[3]) * fm11))
-    e45 = mm(left3(fm0t), rows3(jnp.where(low, corr[4], corr[5]) * fm11))
+    c01, c23, c45 = (jnp.where(low, corr[2 * f], corr[2 * f + 1]) for f in range(3))
+    e01 = mm(fm0p3, rows3(c01 * fm11))
+    e23 = mm(fm03, rows3(c23 * fm11))
+    e45 = mm(fm03, rows3(c45 * fm11))
+    t01 = mm(fm13, rows3(c01 * fm00))
+    t45 = mm(fm1p3, rows3(c45 * fm00))
+
+    def corners(e):
+        lanes = iota(e.shape, 1)
+        ends = jnp.where((lanes == 0) | (lanes == 127), e, 0.0)
+        ends = jnp.where(lanes == 63, pltpu.roll(e, 127, 1), ends)
+        return jnp.where(lanes == 64, pltpu.roll(e, 1, 1), ends)
+
+    def whole(e, side, rows):
+        first, last = rows[0:1], rows[63:64]
+        ends = jnp.where(row == 0, jnp.where(low, first, swap(last)), 0.0)
+        ends = jnp.where(row == 63, jnp.where(low, swap(first), last), ends)
+        return e + corners(side) + ends
+
+    q01 = whole(e01, t45, e23)
+    q23 = whole(e23, e45, e01)
+    q45 = whole(e45, e23, t01)
+    n01, n23, n45 = (jnp.where(last_col, 0.0, pltpu.roll(v, 127, 1)) for v in (q01, q23, q45))
+    d01 = q01 * ((cap01 + 8.2) * q01 - 5.0 * n01)
+    d23 = q23 * ((cap23 + 8.2) * q23 - 5.0 * n23)
+    d45 = q45 * (jnp.where(inner_col, (cap45 + 8.2) * q45, 0.0) - 1.2 * n45)
+    quad = d01 + jnp.where(inner_row, d23 + d45, 0.0)
+    odd = pltpu.roll(q01, 32, 0)
+    after = jnp.where(row < 31, pltpu.roll(q01, 63, 0), 0.0)
+    quad = quad - 1.2 * jnp.where(row < 32, odd * (q01 + after), 0.0)
+    quad = quad - 2.0 * jnp.where(last_row, 0.0, q23 * pltpu.roll(q23, 63, 0))
+    quad = quad - 2.0 * jnp.where(inner_col & jnp.logical_not(last_row), q45 * pltpu.roll(q45, 63, 0), 0.0)
+    quad = quad - jnp.where(low, s_low, s_high) * (e01 * (2.0 * q01 - e01))
+    quad = quad - jnp.where(low, t_low, t_high) * (e23 * (2.0 * q23 - e23))
+    await_halo(0)
+    quad = quad - (2.0 * q01 + l01) * pair(hi_ref[0, 0], hi_ref[0, 1])
+    quad = quad - 0.6 * (2.0 * q23 + l23) * pair(hj_ref[0, 0], hj_ref[0, 1])
+    linear = corr[0] * image_vals[0]
+    for f in range(1, 6):
+        linear = linear + corr[f] * image_vals[f]
+    total = jnp.sum(cacc + quad, keepdims=True) + 2.0 * jnp.sum(linear, keepdims=True)
+    lanes = iota((1, 128), 1)
+    corner = (lanes == 0) | (lanes == 127)
+    corner = corner | (lanes == 63) | (lanes == 64)
+    for at, (across, along) in enumerate(((e23[0:1], e45[0:1]), (e23[63:64], e45[63:64]),
+                                          (e01[0:1], t45[0:1]), (e01[63:64], t45[63:64]))):
+        cs_ref[2 * at : 2 * at + 1, :] = across + corners(along)
+        rest = jnp.where(corner, 0.0, along)
+        if at == 0:
+            rest = jnp.where(lanes == 0, total, jnp.where(lanes == 127, gpart, rest))
+        cs_ref[2 * at + 1 : 2 * at + 2, :] = rest
+    cr_ref[me] = cs_ref[...]
+
+    @peers
+    def _(dd, dev):
+        pltpu.make_async_remote_copy(src_ref=cs_ref, dst_ref=cr_ref.at[me], send_sem=c_s, recv_sem=c_r,
+                                     device_id=dev, device_id_type=MESH).start()
+
     eh, el = split(e45)
     eh = jnp.concatenate([eh, el], axis=0)
 
@@ -315,7 +450,7 @@
         for g in range(CH):
             at = ((c * CH + g) * 64)
             tile = add[:64, g * 128 : g * 128 + 128] + add[64:, g * 128 : g * 128 + 128]
-            p_ref[pl.ds(at + 64, 64), :] = s_ref[pl.ds(at, 64), :] + tile
+            p_ref[pl.ds(at + 64, 64), :] = l_ref[pl.ds(at + 64, 64), :] + tile
 
     p_ref[64:128, :] += jnp.where(low64, e23, 0.0)
     p_ref[T * 64 : T * 64 + 64, :] += jnp.where(low64, 0.0, e23)
@@ -325,91 +460,51 @@
     p_ref[pl.ds(64, 32, stride=64), :] = edge0
     p_ref[pl.ds(64 + 63, 32, stride=64), :] = edge1
 
-    his_ref[0] = edge0
-    his_ref[1] = edge1
-    hjs_ref[0] = p_ref[64:128, :]
-    hjs_ref[1] = p_ref[T * 64 : T * 64 + 64, :]
-
-    sends = (
-        (s > 0, s < nsub - 1, (s - 1, t), his_ref, hi_ref, 0, 1, 0),
-        (s < nsub - 1, s > 0, (s + 1, t), his_ref, hi_ref, 1, 0, 1),
-        (t > 0, t < ncg - 1, (s, t - 1), hjs_ref, hj_ref, 0, 1, 2),
-        (t < ncg - 1, t > 0, (s, t + 1), hjs_ref, hj_ref, 1, 0, 3),
-    )
-
-    def halo(dev, src, dst, a, b, k):
-        return pltpu.make_async_remote_copy(src_ref=src.at[a], dst_ref=dst.at[b], send_sem=h_s.at[k],
-                                            recv_sem=h_r.at[k], device_id=dev, device_id_type=MESH)
-
-    for does, gets, dev, src, dst, a, b, k in sends:
-        @pl.when(does)
-        def _():
-            halo(dev, src, dst, a, b, k).start()
-
-        @pl.when(jnp.logical_not(gets))
-        def _():
-            dst[b] = jnp.zeros(dst.shape[1:], f32)
-
-    ccopy.wait()
     p_ref[0:64, :] = jnp.zeros((64, 128), f32)
     p_ref[(T + 1) * 64 : (T + 2) * 64, :] = jnp.zeros((64, 128), f32)
 
-    row = iota((64, 128), 0)
-    kpos = iota((64, 128), 1) & 63
-
-    def stencil(q, acc):
-        at = pl.multiple_of(q * 64, 64)
-        x = p_ref[pl.ds(at + 64, 64), :]
-        second = swap(x + jnp.where(low64, p_ref[pl.ds(at + 128, 64), :], p_ref[pl.ds(at, 64), :]))
-        up = jnp.where(row == 0, 0.0, pltpu.roll(x, 1, 0))
-        down = jnp.where(row == 63, 0.0, pltpu.roll(x, 63, 0))
-        third = jnp.where(kpos == 0, 0.0, pltpu.roll(x, 1, 1)) + jnp.where(kpos == 63, 0.0, pltpu.roll(x, 127, 1))
-        cols_at = pl.ds(pl.multiple_of(q * 128, 128), 128)
-        img = (cap_ref[:, cols_at] + 8.2) * x - (up + down) - 0.6 * second - 2.5 * third
-        img_out[:, cols_at] = img
-        p_out[:, cols_at] = x
-        return acc + x * img
-
-    cacc = lax.fori_loop(0, T, stencil, jnp.zeros((64, 128), f32), unroll=4)
-    for does, gets, dev, src, dst, a, b, k in sends:
-        @pl.when(gets)
-        def _():
-            halo(dev, src, dst, a, b, k).wait_recv()
-
-    fix0 = 0.6 * jnp.where(low64, swap(hj_ref[0]), 0.0)
-    fix1 = 0.6 * jnp.where(low64, 0.0, swap(hj_ref[1]))
-    cacc = cacc - hjs_ref[0] * fix0 - hjs_ref[1] * fix1
-    csum = his_ref[0] * hi_ref[0] + his_ref[1] * hi_ref[1]
-    cpart = jnp.sum(cacc, axis=0, keepdims=True) - jnp.sum(csum, axis=0, keepdims=True)
-    cpart = jnp.where(low, cpart + swap(cpart), gpart * (1.0 / 64.0))
-    cs_ref[...] = cpart
-    cr_ref[me] = cpart
-
-    @peers
-    def _(dd, dev):
-        pltpu.make_async_remote_copy(src_ref=cs_ref, dst_ref=cr_ref.at[me], send_sem=c_s, recv_sem=c_r,
-                                     device_id=dev, device_id_type=MESH).start()
-
-    img_out[:, :128] = img_out[:, :128] - fix0
-    img_out[:, (T - 1) * 128 :] = img_out[:, (T - 1) * 128 :] - fix1
+    for q in range(T):
+        value, _ = operate(p_ref, q)
+        p_out[:, q * 128 : q * 128 + 128] = value
+    send_halo(1, edge0, edge1, p_ref)
+    await_halo(1)
+    outside = 0.6 * pair(hj_ref[1, 0], hj_ref[1, 1])
+    img_out[:, :128] = img_out[:, :128] - jnp.where(low64, outside, 0.0)
+    img_out[:, (T - 1) * 128 :] = img_out[:, (T - 1) * 128 :] - jnp.where(low64, 0.0, outside)
     for q in range(T):
         at = slice(q * 128, q * 128 + 128)
-        img_out[0:1, at] = img_out[0:1, at] - hi_ref[0, q : q + 1, :]
-        img_out[63:64, at] = img_out[63:64, at] - hi_ref[1, q : q + 1, :]
-
-    pltpu.make_async_copy(cr_ref.at[pl.ds(0, n - 1)], cr_ref.at[pl.ds(0, n - 1)], c_r).wait()
-    both = jnp.sum(cr_ref[...], axis=0)
-    curv = jnp.sum(jnp.where(low, both, 0.0), axis=1, keepdims=True)
-    gamma = jnp.sum(jnp.where(low, 0.0, both), axis=1, keepdims=True)
+        img_out[0:1, at] = img_out[0:1, at] - hi_ref[1, 0, q : q + 1, :]
+        img_out[63:64, at] = img_out[63:64, at] - hi_ref[1, 1, q : q + 1, :]
+
+    arrived(cr_ref, 8, c_r)
+    both = cr_ref[0]
+    first = jnp.zeros((8, 128), f32)
+    second = jnp.zeros((8, 128), f32)
+    for d in range(n):
+        high = pltpu.roll(cr_ref[d], 6, 0)
+        if d > 0:
+            both = both + cr_ref[d]
+        if d + ncg < n:
+            first = first + high * cr_ref[d + ncg]
+        if (d + 1) % ncg:
+            second = second + high * cr_ref[d + 1]
+    row8 = iota((8, 128), 0)
+    lane8 = iota((8, 128), 1)
+    cross = jnp.where(row8 < 2, first, jnp.where((row8 == 4) | (row8 == 5), 0.6 * second, 0.0))
+    inside = ((lane8 & 63) > 0) & ((lane8 & 63) < 63)
+    cross = jnp.where(inside | ((row8 & 1) == 0), -2.0 * cross, 0.0)
+    curv = jnp.sum(cross, keepdims=True) + both[1:2, 0:1]
+    gamma = both[1:2, 127:128]
     alpha_out[...] = gamma / curv
 
     arrived(ag_ref, 6, ag_s)
     arrived(a2r_ref, 6, a2_s)
-    pltpu.make_async_copy(cr_ref.at[pl.ds(0, n - 1)], cr_ref.at[pl.ds(0, n - 1)], c_s).wait()
-    for does, gets, dev, src, dst, a, b, k in sends:
-        @pl.when(does)
-        def _():
-            halo(dev, src, dst, a, b, k).wait_send()
+    arrived(cr_ref, 8, c_s)
+    for turn in range(2):
+        for does, gets, dev, src, dst, a, b, k in sends:
+            @pl.when(does)
+            def _():
+                halo(turn, dev, src, dst, a, b, k).wait_send()
 
 
 def finish(p_ref, img_ref, x_ref, alpha_ref, sol_any, res_any, sol_ref, res_ref, sem):
@@ -460,15 +555,17 @@
             V((n, 8, 128), f32),
             V((nrow, nz, 128), f32),
             V((128 // nz, nz, 128), f32),
-            V((2, 32, 128), f32),
-            V((2, 32, 128), f32),
-            V((2, 64, 128), f32),
-            V((2, 64, 128), f32),
-            V((1, 128), f32),
-            V((n, 1, 128), f32),
+            V((2, 2, 32, 128), f32),
+            V((2, 2, 32, 128), f32),
+            V((2, 2, 32, 128), f32),
+            V((2, 2, 32, 128), f32),
+            V((8, 128), f32),
+            V((n, 8, 128), f32),
+            V(((T + 2) * 64, 128), f32),
+            V((512, 128), f32),
             dma((8,)),
             dma, dma, dma, dma,
-            dma((4,)), dma((4,)),
+            dma((2, 4)), dma((2, 4)),
             dma, dma,
         ],
         compiler_params=pltpu.CompilerParams(collective_id=0, has_side_effects=True,

time: 28.3 us -> 26.4 us (0.933)
  Pallas kernels: 27.5 us -> 25.6 us
    pallas_call x1, Pallas kernels: 25.4 us -> 23.5 us  [body(): pl.pallas_call(functools.partial(kernel, nsub, ncg), out_shape=(field, fi...]
where the time goes in v3:
time: 26.4 us; the launch traced here: 26.2 us
  Pallas kernels  25.6 us (97%)
  between operations  0.64 us (2%)
    pallas_call x1, Pallas kernels, body(): pl.pallas_call(functools.partial(kernel, nsub, ncg), out_shape=(field, fi...  23.5 us
    pallas_call x1, Pallas kernels, body(): pl.pallas_call(finish, out_shape=(field, field), in_specs=[vm] * 4, out_s...  2.08 us

profile of v3, /device:TPU:0, one launch (start us, length us, event | category | flops | bytes accessed | tf_op | source)
XLA Modules:
  0.0 26.2 jit_solution(10170863832206378328)
XLA Ops:
  0.6 23.5 %step.1 = (f32[64,4096]{1,0:T(8,128)S(1)}, f32[64,4096]{1,0:T(8,128)S(1)}, f32[64,4096]{1,0:T(8,128)S(1)}, f32[1,1]{1,0:T(1,128)}) custom-call(f32[64,4096]{1,0:T(8,128)} %x_any.1, f32[3,64,64]{2,1,0:T(8,128)} %modes_any.1, f32[2,64,128]{2,1,0:T(8,128)} %bitcast.2, s32[6,1,128]{2,1,0:T(1,128)} %bitcast.3, s32[6,8]{1,0:T(8,128)} %cols_any.1, ...), custom_call_target="tpu_custom_call" | custom-call | flops 1000000000 | bytes 8388608 | tf_op jit(solution)/shard_map/step/pallas_call | solution.py:533
  24.1 2.1 %finish.1 = (f32[64,4096]{1,0:T(8,128)}, f32[64,4096]{1,0:T(8,128)}) custom-call(f32[64,4096]{1,0:T(8,128)S(1)} %get-tuple-element.6.p_ref, f32[64,4096]{1,0:T(8,128)S(1)} %get-tuple-element.7.img_ref, f32[64,4096]{1,0:T(8,128)S(1)} %get-tuple-element.8.x_ref, f32[1,1]{1,0:T(1,128)} %get-tuple-element.9.alpha_ref), custom_call_target="tpu_custom_call" | custom-call | flops 1048576 | bytes 2097152 | tf_op jit(solution)/shard_map/finish/pallas_call | solution.py:578

commit v4 on v3

--- a/solution.py
+++ b/solution.py
@@ -80,11 +80,11 @@
         return d, (lax.div(d, ncg), lax.rem(d, ncg))
 
     early = [pltpu.make_async_copy(src, dst, dsem.at[k]) for k, (src, dst) in enumerate((
-        (x_any, x_ref), (face_any, face_ref), (map_any, map_ref), (modes_any, modes_ref), (cols_any, cols_ref),
+        (face_any, face_ref), (map_any, map_ref), (x_any, x_ref), (modes_any, modes_ref), (cols_any, cols_ref),
         (wt_any, w_ref), (blk_any, blk_ref), (cap_any, cap_ref)))]
     for copy in early[:5]:
         copy.start()
-    xcopy, fcopy, mcopy, ocopy, lcopy, wcopy, bcopy, ccopy = early
+    fcopy, mcopy, xcopy, ocopy, lcopy, wcopy, bcopy, ccopy = early
 
     def mirror(v, bits):
         out = v
@@ -144,14 +144,32 @@
     dupt = jnp.where((iota((128, 64), 0) & 63) == iota((128, 64), 1), 1.0, 0.0)
     eye128 = jnp.where(iota((128, 128), 0) == iota((128, 128), 1), 1.0, 0.0)
     fm0pt = nn(qm, fm0t)
-    fm0 = fm0t.T
-    fm0p = fm0pt.T
-    fm11 = jnp.concatenate([fm1t, fm1t], axis=0).T
 
     mapf = [(map_ref[f] & 127).astype(f32) for f in range(6)]
     mapf = jnp.concatenate(mapf + [jnp.zeros((2, 128), f32)], axis=0)
     mapt = mmt(eye128.astype(bf16), mapf.astype(bf16))
     lanef = iota((128, 128), 1).astype(f32)
+    hot = [jnp.where(mapt[:, f : f + 1] == lanef, 1.0, 0.0).astype(bf16) for f in range(6)]
+
+    def in_order(mats, faces):
+        m = jnp.concatenate(mats, axis=0)
+        hi, lo = split(m)
+        rest = (m - hi.astype(f32) - lo.astype(f32)).astype(bf16)
+        size = m.shape[0]
+        r = mm(jnp.concatenate([hi, lo, rest], axis=0), jnp.concatenate([hot[f] for f in faces], axis=1))
+        r = r[:size] + r[size : 2 * size] + r[2 * size :]
+        return [r[k * 64 : k * 64 + 64] for k in range(len(mats))]
+
+    def apart(m):
+        zero = jnp.zeros((64, 128), f32)
+        return jnp.concatenate([jnp.concatenate([m[:, :128], zero], axis=1),
+                                jnp.concatenate([zero, m[:, 128:]], axis=1)], axis=0)
+
+    a01, b01 = in_order([fm0pt, fm1t], (0, 1))
+    a25, b25 = in_order([fm0t, fm1t], (2, 3, 4, 5))
+    a23, a45, b23, b45 = a25[:, :256], a25[:, 256:], b25[:, :256], b25[:, 256:]
+    w01, w23, w45 = apart(b01), apart(b23), apart(b45)
+    w01r, w23r, w45r = rows3(w01), rows3(w23), rows3(w45)
 
     xcopy.wait()
     for copy in early[5:]:
@@ -172,17 +190,12 @@
         return f01, f23, f45[:64] + f45[64:]
 
     def restrict(f01, f23, f45):
-        vals = []
-        for left, plane in ((fm0p, f01), (fm0, f23), (fm0, f45)):
-            u = mm(left3(left), rows3(plane)) * fm11
-            vals.append(jnp.sum(jnp.where(low, u, 0.0), axis=1, keepdims=True))
-            vals.append(jnp.sum(jnp.where(low, 0.0, u), axis=1, keepdims=True))
-        return vals
+        return [jnp.sum(mm(left3(plane), w) * a, axis=0, keepdims=True)
+                for plane, w, a in ((f01, w01r, a01), (f23, w23r, a23), (f45, w45r, a45))]
 
     rows = []
-    for f, val in enumerate(restrict(*planes(x_ref))):
-        place = mapt[:, f : f + 1] == lanef
-        rows.append(jnp.sum(jnp.where(place, val, 0.0), axis=0, keepdims=True))
+    for both in restrict(*planes(x_ref)):
+        rows.extend([both[:, :128], both[:, 128:]])
     mine = jnp.concatenate(rows + [jnp.zeros((2, 128), f32)], axis=0)
     send1_ref[...] = mine
     ag_ref[me] = mine
@@ -366,8 +379,11 @@
     l23 = jnp.where(low64, l_ref[64:128, :], l_ref[T * 64 : T * 64 + 64, :])
     image_vals = restrict(*planes(img_out))
 
-    fm00 = jnp.concatenate([fm0t, fm0t], axis=0).T
-    fm0p3, fm03, fm13, fm1p3 = left3(fm0pt), left3(fm0t), left3(fm1t), left3(nn(qm, fm1t))
+    (n01,) = in_order([fm0t], (0, 1))
+    (p45,) = in_order([nn(qm, fm1t)], (4, 5))
+    ends01 = jnp.concatenate([b01[0:8], b01[56:64]], axis=0)
+    x01, x23, x45 = rows3(w01.T), rows3(w23.T), rows3(w45.T)
+    y01, y45 = rows3(apart(n01).T), rows3(apart(a45).T)
     inner_row = (row > 0) & (row < 63)
     inner_col = (kpos > 0) & (kpos < 63)
     last_row = row == 63
@@ -379,16 +395,12 @@
 
     arrived(a2r_ref, 6, a2_r)
     backs = jnp.sum(a2r_ref[...], axis=0)
-    corr = []
-    for f in range(6):
-        place = mapt[:, f : f + 1] == lanef
-        corr.append(jnp.sum(jnp.where(place, backs[f : f + 1], 0.0), axis=1, keepdims=True))
-    c01, c23, c45 = (jnp.where(low, corr[2 * f], corr[2 * f + 1]) for f in range(3))
-    e01 = mm(fm0p3, rows3(c01 * fm11))
-    e23 = mm(fm03, rows3(c23 * fm11))
-    e45 = mm(fm03, rows3(c45 * fm11))
-    t01 = mm(fm13, rows3(c01 * fm00))
-    t45 = mm(fm1p3, rows3(c45 * fm00))
+    v01, v23, v45 = (jnp.concatenate([backs[f : f + 1], backs[f + 1 : f + 2]], axis=1) for f in (0, 2, 4))
+    e01 = mm(left3(a01 * v01), x01)
+    e23 = mm(left3(a23 * v23), x23)
+    e45 = mm(left3(a45 * v45), x45)
+    t01 = mm(left3(ends01 * v01), y01)
+    t45 = mm(left3(p45 * v45), y45)
 
     def corners(e):
         lanes = iota(e.shape, 1)
@@ -396,19 +408,18 @@
         ends = jnp.where(lanes == 63, pltpu.roll(e, 127, 1), ends)
         return jnp.where(lanes == 64, pltpu.roll(e, 1, 1), ends)
 
-    def whole(e, side, rows):
-        first, last = rows[0:1], rows[63:64]
+    def whole(e, side, first, last):
         ends = jnp.where(row == 0, jnp.where(low, first, swap(last)), 0.0)
         ends = jnp.where(row == 63, jnp.where(low, swap(first), last), ends)
         return e + corners(side) + ends
 
-    q01 = whole(e01, t45, e23)
-    q23 = whole(e23, e45, e01)
-    q45 = whole(e45, e23, t01)
-    n01, n23, n45 = (jnp.where(last_col, 0.0, pltpu.roll(v, 127, 1)) for v in (q01, q23, q45))
-    d01 = q01 * ((cap01 + 8.2) * q01 - 5.0 * n01)
-    d23 = q23 * ((cap23 + 8.2) * q23 - 5.0 * n23)
-    d45 = q45 * (jnp.where(inner_col, (cap45 + 8.2) * q45, 0.0) - 1.2 * n45)
+    q01 = whole(e01, t45, e23[0:1], e23[63:64])
+    q23 = whole(e23, e45, e01[0:1], e01[63:64])
+    q45 = whole(e45, e23, t01[0:1], t01[15:16])
+    k01, k23, k45 = (jnp.where(last_col, 0.0, pltpu.roll(v, 127, 1)) for v in (q01, q23, q45))
+    d01 = q01 * ((cap01 + 8.2) * q01 - 5.0 * k01)
+    d23 = q23 * ((cap23 + 8.2) * q23 - 5.0 * k23)
+    d45 = q45 * (jnp.where(inner_col, (cap45 + 8.2) * q45, 0.0) - 1.2 * k45)
     quad = d01 + jnp.where(inner_row, d23 + d45, 0.0)
     odd = pltpu.roll(q01, 32, 0)
     after = jnp.where(row < 31, pltpu.roll(q01, 63, 0), 0.0)
@@ -420,9 +431,7 @@
     await_halo(0)
     quad = quad - (2.0 * q01 + l01) * pair(hi_ref[0, 0], hi_ref[0, 1])
     quad = quad - 0.6 * (2.0 * q23 + l23) * pair(hj_ref[0, 0], hj_ref[0, 1])
-    linear = corr[0] * image_vals[0]
-    for f in range(1, 6):
-        linear = linear + corr[f] * image_vals[f]
+    linear = v01 * image_vals[0] + v23 * image_vals[1] + v45 * image_vals[2]
     total = jnp.sum(cacc + quad, keepdims=True) + 2.0 * jnp.sum(linear, keepdims=True)
     lanes = iota((1, 128), 1)
     corner = (lanes == 0) | (lanes == 127)
@@ -508,18 +517,15 @@
 
 
 def finish(p_ref, img_ref, x_ref, alpha_ref, sol_any, res_any, sol_ref, res_ref, sem):
-    copies = []
     a = alpha_ref[...]
-    for c in range(8):
-        at = pl.ds(c * 8, 8)
+    for c in range(4):
+        at = pl.ds(c * 16, 16)
         sol_ref[at, :] = a * p_ref[at, :]
-        copies.append(pltpu.make_async_copy(sol_ref.at[at], sol_any.at[at], sem.at[0, c]))
-        copies[-1].start()
+        pltpu.make_async_copy(sol_ref.at[at], sol_any.at[at], sem.at[0]).start()
         res_ref[at, :] = x_ref[at, :] - a * img_ref[at, :]
-        copies.append(pltpu.make_async_copy(res_ref.at[at], res_any.at[at], sem.at[1, c]))
-        copies[-1].start()
-    for copy in copies:
-        copy.wait()
+        pltpu.make_async_copy(res_ref.at[at], res_any.at[at], sem.at[1]).start()
+    pltpu.make_async_copy(sol_ref, sol_any, sem.at[0]).wait()
+    pltpu.make_async_copy(res_ref, res_any, sem.at[1]).wait()
 
 
 def body(nsub, ncg, source, capacity, fd_weights, fd_modes, face_modes, coarse_map, fsai_cols, fsai_blocks):
@@ -580,7 +586,7 @@
         out_shape=(field, field),
         in_specs=[vm] * 4,
         out_specs=(hbm, hbm),
-        scratch_shapes=[V(source.shape, f32), V(source.shape, f32), dma((2, 8))],
+        scratch_shapes=[V(source.shape, f32), V(source.shape, f32), dma((2,))],
         cost_estimate=pl.CostEstimate(flops=2**20, bytes_accessed=2 * 2**20, transcendentals=0),
         name="finish",
     )(*(pltpu.with_memory_space_constraint(v, pltpu.VMEM) for v in (p, img, x, alpha)))

time: 26.4 us -> 26.2 us (level)
  no operation moved by 1% of the time
where the time goes in v4:
time: 26.2 us; the launch traced here: 26.1 us
  Pallas kernels  25.4 us (97%)
  between operations  0.64 us (2%)
    pallas_call x1, Pallas kernels, body(): pl.pallas_call(functools.partial(kernel, nsub, ncg), out_shape=(field, fi...  23.5 us
    pallas_call x1, Pallas kernels, body(): pl.pallas_call(finish, out_shape=(field, field), in_specs=[vm] * 4, out_s...  1.97 us

profile of v4, /device:TPU:0, one launch (start us, length us, event | category | flops | bytes accessed | tf_op | source)
XLA Modules:
  0.0 26.1 jit_solution(14465502737460133984)
XLA Ops:
  0.6 23.5 %step.1 = (f32[64,4096]{1,0:T(8,128)S(1)}, f32[64,4096]{1,0:T(8,128)S(1)}, f32[64,4096]{1,0:T(8,128)S(1)}, f32[1,1]{1,0:T(1,128)}) custom-call(f32[64,4096]{1,0:T(8,128)} %x_any.1, f32[3,64,64]{2,1,0:T(8,128)} %modes_any.1, f32[2,64,128]{2,1,0:T(8,128)} %bitcast.2, s32[6,1,128]{2,1,0:T(1,128)} %bitcast.3, s32[6,8]{1,0:T(8,128)} %cols_any.1, ...), custom_call_target="tpu_custom_call" | custom-call | flops 1000000000 | bytes 8388608 | tf_op jit(solution)/shard_map/step/pallas_call | solution.py:539
  24.1 2.0 %finish.1 = (f32[64,4096]{1,0:T(8,128)}, f32[64,4096]{1,0:T(8,128)}) custom-call(f32[64,4096]{1,0:T(8,128)S(1)} %get-tuple-element.6.p_ref, f32[64,4096]{1,0:T(8,128)S(1)} %get-tuple-element.7.img_ref, f32[64,4096]{1,0:T(8,128)S(1)} %get-tuple-element.8.x_ref, f32[1,1]{1,0:T(1,128)} %get-tuple-element.9.alpha_ref), custom_call_target="tpu_custom_call" | custom-call | flops 1048576 | bytes 2097152 | tf_op jit(solution)/shard_map/finish/pallas_call | solution.py:584

commit v5 on v4

--- a/solution.py
+++ b/solution.py
@@ -67,9 +67,9 @@
            p_out, img_out, x_ref, alpha_out,
            modes_ref, face_ref, map_ref, cols_ref,
            s_ref, z_ref, w_ref, p_ref, cap_ref, blk_ref, sel_ref, am_ref, kw_ref,
-           ag_ref, send1_ref, a2s_ref, a2r_ref, pick_ref, spread_ref,
+           ag_ref, send1_ref, a2s_ref, a2r_ref,
            hi_ref, his_ref, hj_ref, hjs_ref, cs_ref, cr_ref, l_ref, strip_ref,
-           dsem, ag_s, ag_r, a2_s, a2_r, h_s, h_r, c_s, c_r):
+           dsem, out_s, ag_r, a2_r, h_r, c_r):
     n = nsub * ncg
     s = lax.axis_index("sub")
     t = lax.axis_index("cgrp")
@@ -86,12 +86,18 @@
         copy.start()
     fcopy, mcopy, xcopy, ocopy, lcopy, wcopy, bcopy, ccopy = early
 
-    def mirror(v, bits):
-        out = v
-        for k in range(8):
-            if bits >> k & 1:
-                out = out + (1 << k) - (2 << k) * lax.rem(lax.div(v, 1 << k), 2)
+    def mirrors(v, size):
+        out = [v]
+        while len(out) < size:
+            bit = len(out)
+            flip = bit - 2 * bit * lax.rem(lax.div(v, bit), 2)
+            out = out + [o + flip for o in out]
         return out
+
+    if n <= 32:
+        to_s, to_t = mirrors(s, nsub), mirrors(t, ncg)
+        order = [(a, b) for a in range(nsub) for b in range(ncg) if a or b]
+        order.sort(key=lambda ab: -(min(ab[0], 2) + (ab[1] >> 1 & 1) + (ab[1] >> 2 & 1)))
 
     def peers(step):
         if n > 32:
@@ -99,10 +105,8 @@
             def _(o):
                 step(*peer(o))
         else:
-            pairs = [(a, b) for a in range(nsub) for b in range(ncg) if a or b]
-            for a, b in sorted(pairs, key=lambda ab: -(ab[0] + (ab[1] >> 1 & 1) + (ab[1] >> 2 & 1))):
-                ds, dt = mirror(s, a), mirror(t, b)
-                step(ds * ncg + dt, (ds, dt))
+            for a, b in order:
+                step(to_s[a] * ncg + to_t[b], (to_s[a], to_t[b]))
 
     def arrived(ref, rows, sem):
         part = ref.at[pl.ds(0, n - 1), pl.ds(0, rows)]
@@ -205,7 +209,7 @@
     @peers
     def _(dd, dev):
         pltpu.make_async_remote_copy(src_ref=send1_ref.at[pl.ds(0, 6)], dst_ref=ag_ref.at[me, pl.ds(0, 6)],
-                                     send_sem=ag_s, recv_sem=ag_r,
+                                     send_sem=out_s, recv_sem=ag_r,
                                      device_id=dev, device_id_type=MESH).start()
 
     ocopy.wait()
@@ -273,36 +277,38 @@
 
     g2 = g1.T.astype(bf16)
     g2 = jnp.concatenate([g2, g2], axis=1)
-    g1 = g1.astype(bf16)
+    g1 = g1.astype(bf16)[: -(-kk // 16) * 16]
+    bcopy.wait()
 
     arrived(ag_ref, 6, ag_r)
-    th, tl = split(ag_ref[...].reshape(n * 8, 128))
-    picked = mm(g1, th) + mm(g1, tl)
-    pick_ref[...] = picked[:kk].reshape(nrow, nz, 128)
-    bcopy.wait()
-    spread_ref[...] = jnp.zeros_like(spread_ref)
-
-    def coarse_row(i, acc):
-        pk = pick_ref[i]
-        tot = blk_ref[i, 0] * pk[0:1]
-        for k in range(1, nz):
-            tot = tot + blk_ref[i, k] * pk[k : k + 1]
-        img = jnp.sum(tot, axis=1, keepdims=True)
-        out = [jnp.sum(blk_ref[i, k] * img, axis=0, keepdims=True) for k in range(nz)]
-        spread_ref[i] = jnp.concatenate(out, axis=0)
-        return acc + img * img
-
-    iacc = jnp.zeros((128, 1), f32)
+    picked = mm(g1, jnp.concatenate(split(ag_ref[...].reshape(n * 8, 128)), axis=1))
+    picked = picked[:kk, :128] + picked[:kk, 128:]
+
+    iacc = jnp.zeros((16, 1), f32)
+    spread = []
     for i in range(nrow):
-        iacc = coarse_row(i, iacc)
-    back = mm(g2, jnp.concatenate(split(spread_ref[...].reshape(128, 128)), axis=0))
+        pk = picked[i * nz : i * nz + nz]
+        out = [jnp.zeros((16, 128), f32)] * nz
+        for at in range(0, 128, 16):
+            part = [blk_ref[i, k, at : at + 16, :] for k in range(nz)]
+            tot = part[0] * pk[0:1]
+            for k in range(1, nz):
+                tot = tot + part[k] * pk[k : k + 1]
+            img = jnp.sum(tot, axis=1, keepdims=True)
+            iacc = iacc + img * img
+            out = [o + v * img for o, v in zip(out, part)]
+        spread.extend(jnp.sum(o, axis=0, keepdims=True) for o in out)
+    spread = jnp.concatenate(spread + [jnp.zeros((128 - kk, 128), f32)], axis=0)
+    back = mm(g2, jnp.concatenate(split(spread), axis=0))
     a2s_ref[...] = back.reshape(n, 8, 128)
     a2r_ref[me] = a2s_ref[me]
+
+    arrived(ag_ref, 6, out_s)
 
     @peers
     def _(dd, dev):
         pltpu.make_async_remote_copy(src_ref=a2s_ref.at[dd, pl.ds(0, 6)], dst_ref=a2r_ref.at[me, pl.ds(0, 6)],
-                                     send_sem=a2_s, recv_sem=a2_r,
+                                     send_sem=out_s, recv_sem=a2_r,
                                      device_id=dev, device_id_type=MESH).start()
 
     gpart = jnp.sum(iacc, keepdims=True) + jnp.sum(gacc, keepdims=True)
@@ -343,7 +349,7 @@
     )
 
     def halo(turn, dev, src, dst, a, b, k):
-        return pltpu.make_async_remote_copy(src_ref=src.at[turn, a], dst_ref=dst.at[turn, b], send_sem=h_s.at[turn, k],
+        return pltpu.make_async_remote_copy(src_ref=src.at[turn, a], dst_ref=dst.at[turn, b], send_sem=dsem.at[4 * turn + k],
                                             recv_sem=h_r.at[turn, k], device_id=dev, device_id_type=MESH)
 
     def send_halo(turn, edge0, edge1, ref):
@@ -445,10 +451,22 @@
         cs_ref[2 * at + 1 : 2 * at + 2, :] = rest
     cr_ref[me] = cs_ref[...]
 
+    arrived(a2r_ref, 6, out_s)
+
+    def send_sum(dd, dev):
+        pltpu.make_async_remote_copy(src_ref=cs_ref, dst_ref=cr_ref.at[me], send_sem=out_s, recv_sem=c_r,
+                                     device_id=dev, device_id_type=MESH).start()
+
+    for d in range(ncg):
+        @pl.when(me != d)
+        def _():
+            send_sum(d, (0, d))
+
     @peers
     def _(dd, dev):
-        pltpu.make_async_remote_copy(src_ref=cs_ref, dst_ref=cr_ref.at[me], send_sem=c_s, recv_sem=c_r,
-                                     device_id=dev, device_id_type=MESH).start()
+        @pl.when(dd >= ncg)
+        def _():
+            send_sum(dd, dev)
 
     eh, el = split(e45)
     eh = jnp.concatenate([eh, el], axis=0)
@@ -506,9 +524,7 @@
     gamma = both[1:2, 127:128]
     alpha_out[...] = gamma / curv
 
-    arrived(ag_ref, 6, ag_s)
-    arrived(a2r_ref, 6, a2_s)
-    arrived(cr_ref, 8, c_s)
+    arrived(cr_ref, 8, out_s)
     for turn in range(2):
         for does, gets, dev, src, dst, a, b, k in sends:
             @pl.when(does)
@@ -559,8 +575,6 @@
             V((8, 128), f32),
             V((n, 8, 128), f32),
             V((n, 8, 128), f32),
-            V((nrow, nz, 128), f32),
-            V((128 // nz, nz, 128), f32),
             V((2, 2, 32, 128), f32),
             V((2, 2, 32, 128), f32),
             V((2, 2, 32, 128), f32),
@@ -570,9 +584,7 @@
             V(((T + 2) * 64, 128), f32),
             V((512, 128), f32),
             dma((8,)),
-            dma, dma, dma, dma,
-            dma((2, 4)), dma((2, 4)),
-            dma, dma,
+            dma, dma, dma, dma((2, 4)), dma,
         ],
         compiler_params=pltpu.CompilerParams(collective_id=0, has_side_effects=True,
                                              vmem_limit_bytes=48 * 1024 * 1024),

time: 26.2 us -> 25.3 us (0.966)
  Pallas kernels: 25.4 us -> 24.5 us
    pallas_call x1, Pallas kernels: 23.5 us -> 22.5 us  [body(): pl.pallas_call(functools.partial(kernel, nsub, ncg), out_shape=(field, fi...]
where the time goes in v5:
time: 25.3 us; the launch traced here: 25.1 us
  Pallas kernels  24.5 us (97%)
  between operations  0.64 us (3%)
    pallas_call x1, Pallas kernels, body(): pl.pallas_call(functools.partial(kernel, nsub, ncg), out_shape=(field, fi...  22.5 us
    pallas_call x1, Pallas kernels, body(): pl.pallas_call(finish, out_shape=(field, field), in_specs=[vm] * 4, out_s...  1.97 us

profile of v5, /device:TPU:0, one launch (start us, length us, event | category | flops | bytes accessed | tf_op | source)
XLA Modules:
  0.0 25.1 jit_solution(957668548893623501)
XLA Ops:
  0.6 22.5 %step.1 = (f32[64,4096]{1,0:T(8,128)S(1)}, f32[64,4096]{1,0:T(8,128)S(1)}, f32[64,4096]{1,0:T(8,128)S(1)}, f32[1,1]{1,0:T(1,128)}) custom-call(f32[64,4096]{1,0:T(8,128)} %x_any.1, f32[3,64,64]{2,1,0:T(8,128)} %modes_any.1, f32[2,64,128]{2,1,0:T(8,128)} %bitcast.2, s32[6,1,128]{2,1,0:T(1,128)} %bitcast.3, s32[6,8]{1,0:T(8,128)} %cols_any.1, ...), custom_call_target="tpu_custom_call" | custom-call | flops 1000000000 | bytes 8388608 | tf_op jit(solution)/shard_map/step/pallas_call | solution.py:555
  23.1 2.0 %finish.1 = (f32[64,4096]{1,0:T(8,128)}, f32[64,4096]{1,0:T(8,128)}) custom-call(f32[64,4096]{1,0:T(8,128)S(1)} %get-tuple-element.6.p_ref, f32[64,4096]{1,0:T(8,128)S(1)} %get-tuple-element.7.img_ref, f32[64,4096]{1,0:T(8,128)S(1)} %get-tuple-element.8.x_ref, f32[1,1]{1,0:T(1,128)} %get-tuple-element.9.alpha_ref), custom_call_target="tpu_custom_call" | custom-call | flops 1048576 | bytes 2097152 | tf_op jit(solution)/shard_map/finish/pallas_call | solution.py:596

commit v6 on v5

--- a/solution.py
+++ b/solution.py
@@ -400,7 +400,12 @@
     t_high = jnp.where(t < ncg - 1, 0.6, 0.0)
 
     arrived(a2r_ref, 6, a2_r)
-    backs = jnp.sum(a2r_ref[...], axis=0)
+    def total_of(parts):
+        while len(parts) > 1:
+            parts = [sum(parts[k : k + 2][1:], parts[k]) for k in range(0, len(parts), 2)]
+        return parts[0]
+
+    backs = total_of([a2r_ref[d] for d in range(n)])
     v01, v23, v45 = (jnp.concatenate([backs[f : f + 1], backs[f + 1 : f + 2]], axis=1) for f in (0, 2, 4))
     e01 = mm(left3(a01 * v01), x01)
     e23 = mm(left3(a23 * v23), x23)
@@ -504,17 +509,11 @@
         img_out[63:64, at] = img_out[63:64, at] - hi_ref[1, 1, q : q + 1, :]
 
     arrived(cr_ref, 8, c_r)
-    both = cr_ref[0]
-    first = jnp.zeros((8, 128), f32)
-    second = jnp.zeros((8, 128), f32)
-    for d in range(n):
-        high = pltpu.roll(cr_ref[d], 6, 0)
-        if d > 0:
-            both = both + cr_ref[d]
-        if d + ncg < n:
-            first = first + high * cr_ref[d + ncg]
-        if (d + 1) % ncg:
-            second = second + high * cr_ref[d + 1]
+    got = [cr_ref[d] for d in range(n)]
+    high = [pltpu.roll(v, 6, 0) for v in got]
+    both = total_of(got)
+    first = total_of([high[d] * got[d + ncg] for d in range(n - ncg)])
+    second = total_of([high[d] * got[d + 1] for d in range(n) if (d + 1) % ncg])
     row8 = iota((8, 128), 0)
     lane8 = iota((8, 128), 1)
     cross = jnp.where(row8 < 2, first, jnp.where((row8 == 4) | (row8 == 5), 0.6 * second, 0.0))

time: 25.3 us -> 25.2 us (level)
  no operation moved by 1% of the time
where the time goes in v6:
time: 25.2 us; the launch traced here: 25.1 us
  Pallas kernels  24.4 us (97%)
  between operations  0.64 us (3%)
    pallas_call x1, Pallas kernels, body(): pl.pallas_call(functools.partial(kernel, nsub, ncg), out_shape=(field, fi...  22.5 us
    pallas_call x1, Pallas kernels, body(): pl.pallas_call(finish, out_shape=(field, field), in_specs=[vm] * 4, out_s...  1.97 us

profile of v6, /device:TPU:0, one launch (start us, length us, event | category | flops | bytes accessed | tf_op | source)
XLA Modules:
  0.0 25.1 jit_solution(10789690138988204118)
XLA Ops:
  0.6 22.5 %step.1 = (f32[64,4096]{1,0:T(8,128)S(1)}, f32[64,4096]{1,0:T(8,128)S(1)}, f32[64,4096]{1,0:T(8,128)S(1)}, f32[1,1]{1,0:T(1,128)}) custom-call(f32[64,4096]{1,0:T(8,128)} %x_any.1, f32[3,64,64]{2,1,0:T(8,128)} %modes_any.1, f32[2,64,128]{2,1,0:T(8,128)} %bitcast.2, s32[6,1,128]{2,1,0:T(1,128)} %bitcast.3, s32[6,8]{1,0:T(8,128)} %cols_any.1, ...), custom_call_target="tpu_custom_call" | custom-call | flops 1000000000 | bytes 8388608 | tf_op jit(solution)/shard_map/step/pallas_call | solution.py:554
  23.1 2.0 %finish.1 = (f32[64,4096]{1,0:T(8,128)}, f32[64,4096]{1,0:T(8,128)}) custom-call(f32[64,4096]{1,0:T(8,128)S(1)} %get-tuple-element.6.p_ref, f32[64,4096]{1,0:T(8,128)S(1)} %get-tuple-element.7.img_ref, f32[64,4096]{1,0:T(8,128)S(1)} %get-tuple-element.8.x_ref, f32[1,1]{1,0:T(1,128)} %get-tuple-element.9.alpha_ref), custom_call_target="tpu_custom_call" | custom-call | flops 1048576 | bytes 2097152 | tf_op jit(solution)/shard_map/finish/pallas_call | solution.py:595
